TPU v7x, 256 devices: a whole 4x4x8 slice. The times are simulated.
256 devices in a mesh: box: 64 (over y, z, x_lo), blk: 4 (over x_hi, core).
Axes of the slice: x: 4 (x_hi: 2, x_lo: 2; x = x_hi * 2 + x_lo), y: 4, z: 8, core: 2. Of those that a mesh axis runs over, the one named last changes fastest.
Arguments:
- panels: float32 [1024, 4, 256], P('box'), may hold values from 0 to 65, as said below
- self_blocks: float32 [1024, 256, 256], P('box'), may hold values from 0 to 8, as said below
- neighbors: int32 [1024, 8], P('box'), may hold values from 0 to 1023, as said below
- skeleton_one: int32 [1024, 128], P('box'), may hold values from 0 to 255, as said below
- count_one: int32 [1024], P('box'), may hold values from 64 to 128
- skeleton_two: int32 [512, 128], P('box'), may hold values from 0 to 255, as said below
- count_two: int32 [512], P('box'), may hold values from 64 to 128
- parent_at_slot: int32 [512], P('box'), may hold values from 0 to 511, as said below
Outputs:
- level_one: float32 [1024, 128, 128], P('box', 'blk')
- level_two: float32 [512, 128, 128], P('box', 'blk')
Inputs may be any that keep to these rules, and one draw needn't show every extreme that they name: `neighbors`: each box's 8 neighbours are distinct other boxes whose index differs from its own by at most 16; one of them differs by exactly 16. `skeleton_one`: each row lists 128 distinct panel positions. `skeleton_two`: each row lists 128 distinct positions. `parent_at_slot`: a permutation of the parents. `panels`: self terms (component 3) are 1 or more. `self_blocks`: diagonal entries equal the panels' self terms; the other entries are positive.
All inputs are finite; a program needn't handle non-finite values. Where the computation divides by a largest or mean magnitude, that divisor is 1e-20 or more.
Results may differ from a plain program's by a relative error of at most 0.0003.
Values sent between devices are 32-bit elements; how exact they have to be, the bound alone decides.
A program may use at most 128 MiB of HBM per device.

v0:
```python
import jax
import jax.numpy as jnp
from jax import lax
from jax.sharding import PartitionSpec as P

STEPS = 3


precise = lax.Precision.HIGHEST


def with_halo(cells, sides, width):
    for axis, dim in sides:
        count = lax.axis_size(axis)
        ends = count - 1
        head = lax.slice_in_dim(cells, 0, width, axis=dim)
        tail = lax.slice_in_dim(cells, cells.shape[dim] - width, cells.shape[dim], axis=dim)
        cells = jnp.concatenate(
            [
                lax.ppermute(tail, axis, [(i, (i + 1) % count) for i in range(ends)]),
                cells,
                lax.ppermute(head, axis, [((i + 1) % count, i) for i in range(ends)]),
            ],
            axis=dim,
        )
    return cells


def kernel(source, target):
    parts = []
    for axis_id in range(3):
        offset = source[..., axis_id, :, None] - target[..., axis_id, None, :]
        parts.append(offset * offset)
    return 0.03125 / jnp.sqrt(parts[0] + parts[1] + parts[2] + 0.01)


def normal_terms(proxy_kernel, skeleton, live_mask):
    picked_cols = jnp.take(proxy_kernel, skeleton, axis=1) * live_mask[None, :]
    gram_part = jnp.dot(picked_cols.T, picked_cols, precision=precise)
    right_part = jnp.dot(picked_cols.T, proxy_kernel, precision=precise)
    return (gram_part, right_part)


def refine(gram_part, right_part, skeleton, live_mask):
    step_size = 1.0 / jnp.max(jnp.sum(jnp.abs(gram_part), axis=-1), axis=-1)
    fits = jax.nn.one_hot(skeleton, right_part.shape[-1], dtype=jnp.float32) * live_mask[..., None]
    for sweep in range(STEPS):
        update = right_part - jnp.einsum("...kl,...lp->...kp", gram_part, fits, precision=precise)
        fits = fits + step_size[..., None, None] * update
    return fits


def local(
    panels, self_blocks, neighbors, skeleton_one, count_one, skeleton_two, count_two, parent_at_slot
):
    box_count = panels.shape[0]
    pair_count = box_count // 2
    slot_count = skeleton_one.shape[1]
    blk_count = lax.axis_size("blk")
    member_id = lax.axis_index("blk")
    home_id = lax.axis_index("box")
    row_share = slot_count // blk_count
    near_share = neighbors.shape[1] // blk_count
    slot_ids = jnp.arange(slot_count)
    panel_window = with_halo(panels, (("box", 0),), box_count)
    local_near = neighbors - (home_id - 1) * box_count
    live_one = (slot_ids[None, :] < count_one[:, None]).astype(jnp.float32)
    mine_near = lax.dynamic_slice_in_dim(local_near, member_id * near_share, near_share, 1)

    def proxy_terms(box_id, near_ids):
        near_pts = panel_window[near_ids, :3]
        proxy = jnp.transpose(near_pts, (1, 0, 2)).reshape(3, -1)
        proxy_kernel = kernel(proxy, panels[box_id, :3])
        return normal_terms(proxy_kernel, skeleton_one[box_id], live_one[box_id])

    gram_part, right_part = lax.map(
        lambda box_id: proxy_terms(box_id, mine_near[box_id]), jnp.arange(box_count)
    )
    gram_part, right_part = lax.psum((gram_part, right_part), "blk")
    fits = refine(gram_part, right_part, skeleton_one, live_one)
    far_fits = with_halo(fits, (("box", 0),), box_count)

    def coarse(box_id):
        own_fit = fits[box_id]
        own_rows = lax.dynamic_slice_in_dim(own_fit, member_id * row_share, row_share, 0)
        block_rows = jnp.dot(
            jnp.dot(own_rows, self_blocks[box_id], precision=precise), own_fit.T, precision=precise
        )
        near_cols = mine_near[box_id]
        near_fits = far_fits[near_cols]
        weight = jnp.maximum(
            jnp.einsum(
                "nkp,np->nk", near_fits * near_fits, panel_window[near_cols, 3], precision=precise
            ),
            1.0,
        )
        couple = kernel(panels[box_id, :3], panel_window[near_cols, :3])
        left_prod = jnp.einsum("kp,npq->nkq", own_fit, couple, precision=precise)
        cross_block = jnp.einsum("nkq,nlq->nkl", left_prod, near_fits, precision=precise)
        schur_term = jnp.einsum(
            "nkl,nml->km", cross_block / weight[:, None, :], cross_block, precision=precise
        )
        return (block_rows, schur_term)

    block_rows, schur_term = lax.map(coarse, jnp.arange(box_count))
    schur_rows = lax.psum_scatter(schur_term, "blk", scatter_dimension=1, tiled=True)
    level_one = block_rows - schur_rows

    def sibling(pair_id):
        first = 2 * pair_id
        second = first + 1
        couple = kernel(panels[first, :3], panels[second, :3])
        first_rows = lax.dynamic_slice_in_dim(fits[first], member_id * row_share, row_share, 0)
        second_rows = lax.dynamic_slice_in_dim(fits[second], member_id * row_share, row_share, 0)
        upper_rows = jnp.dot(
            jnp.dot(first_rows, couple, precision=precise), fits[second].T, precision=precise
        )
        lower_rows = jnp.dot(
            jnp.dot(second_rows, couple.T, precision=precise), fits[first].T, precision=precise
        )
        return jnp.concatenate(
            [
                jnp.concatenate([level_one[first], upper_rows], 1),
                jnp.concatenate([lower_rows, level_one[second]], 1),
            ],
            0,
        )

    flat_blocks = lax.map(sibling, jnp.arange(pair_count)).reshape(pair_count, -1)
    empty_sum = jnp.zeros(flat_blocks.shape, jnp.float32)
    shard_rows = jax.tree.map(
        lambda part: lax.all_gather(part, "box", axis=0, tiled=True), flat_blocks
    )
    parent_ids = jnp.arange(shard_rows.shape[0])
    hit_table = (parent_at_slot[:, None] == parent_ids[None, :]).astype(jnp.float32)
    gathered = empty_sum + jnp.dot(hit_table, shard_rows, precision=precise)
    merged = gathered.reshape(pair_count, 2 * row_share, 2 * slot_count)
    live_two = (slot_ids[None, :] < count_two[:, None]).astype(jnp.float32)
    gram_two, right_two = jax.vmap(normal_terms)(merged, skeleton_two, live_two)
    gram_two, right_two = lax.psum((gram_two, right_two), "blk")
    inner_fit = refine(gram_two, right_two, skeleton_two, live_two)
    columns = jnp.concatenate(
        [
            member_id * row_share + jnp.arange(row_share),
            slot_count + member_id * row_share + jnp.arange(row_share),
        ]
    )
    picked = jnp.take(inner_fit, columns, axis=2)
    reduced = jnp.einsum("skr,src->skc", picked, merged, precision=precise)
    parent_term = jnp.einsum("skc,slc->skl", reduced, inner_fit, precision=precise)
    level_two = lax.psum_scatter(parent_term, "blk", scatter_dimension=1, tiled=True)
    return (level_one, level_two)


def solution(mesh):
    placed = (
        P("box", None, None),
        P("box", None, None),
        P("box", None),
        P("box", None),
        P("box"),
        P("box", None),
        P("box"),
        P("box"),
    )
    return jax.shard_map(
        local,
        mesh=mesh,
        in_specs=placed,
        out_specs=(P("box", "blk", None), P("box", "blk", None)),
        check_vma=False,
    )
```

profile of v0, /device:TPU:2, one launch (start us, length us, event | category | flops | bytes accessed | tf_op | source)
XLA Modules:
  0.0 1476.0 jit_solution(2431590176020156388)
XLA Ops:
  8.1 3.8 collective-permute-start
  11.9 2.0 collective-permute-start.1
  16.3 2.6 collective-permute-done.1
  19.0 135.7 %while.43 = (s32[]{:T(128)}, f32[16,128,128]{2,1,0:T(8,128)S(1)}, f32[16,128,256]{2,1,0:T(8,128)}, s32[16]{0:T(128)S(1)}, s32[16,128]{1,0:T(8,128)}, /*index=5*/...) while((s32[]{:T(128)}, f32[16,128,128]{2,1,0:T(8,128)S(1)}, ...), condition=%wide.region_1.2_spmd.clone, body=%wide.region_0.1_spmd.sunk.clone | while | flops 304875648 | bytes 1841123 | solution.py:76
  25.5 1.6 fusion.236
  42.5 1.6 fusion.236
  59.4 1.6 fusion.236
  84.9 1.6 fusion.236
  127.3 1.6 fusion.236
  152.7 1.5 fusion.236
  155.8 83.3 %all-reduce.10.cloned.1.call-done = (f32[16,128,256]{2,1,0:T(8,128)}, f32[16,128,128]{2,1,0:T(8,128)}) async-done(((f32[16,128,256]{2,1,0:T(8,128)}, f32[16,128,128]{2,1,0:T(8,128)}), (f32[16,128,256]{2,1,0:T(8,128)}, f32[16,128,128]{2,1,0:T(8,128)})) %all-reduce.10.cloned.1.call-update) | async-done | bytes 3145744 | tf_op jit(solution)/shard_map/psum | solution.py:79
  239.1 1.6 abs_reduce_fusion
  240.8 4.4 select_add_fusion
  245.2 1.9 fusion.143
  247.1 2.8 multiply_add_fusion
  249.9 4.4 collective-permute-start.2
  254.2 2.9 collective-permute-start.3
  257.1 87.4 %collective-permute-done.2 = f32[16,128,256]{2,1,0:T(8,128)} collective-permute-done((f32[16,128,256]{2,1,0:T(8,128)S(1)}, f32[16,128,256]{2,1,0:T(8,128)}, u32[]{:S(2)}, u32[]{:S(2)}) %collective-permute-start.2) | collective-permute-done | bytes 2097184 | tf_op jit(solution)/shard_map/ppermute | solution.py:20
  344.5 1.9 collective-permute-done.3
  346.5 5.4 pad_maximum_fusion
  353.0 198.0 %while.44 = (s32[]{:T(128)}, f32[16,32,128]{2,1,0:T(8,128)S(1)}, f32[16,128,128]{2,1,0:T(8,128)}, s32[16]{0:T(128)S(1)}, f32[16,128,256]{2,1,0:T(8,128)S(1)}, /*...) while((s32[]{:T(128)}, f32[16,32,128]{2,1,0:T(8,128)S(1)}, ...), condition=%wide.region_7.8_spmd.clone, body=%wide.region_6.7_spmd.sunk.clone | while | flops 392267008 | bytes 3119423 | solution.py:105
  358.2 3.3 gather_fusion.3
  370.5 3.3 gather_fusion.3
  382.9 3.3 gather_fusion.3
  395.3 3.3 gather_fusion.3
  407.7 3.3 gather_fusion.3
  420.0 3.3 gather_fusion.3
  432.4 3.3 gather_fusion.3
  444.8 3.3 gather_fusion.3
  457.1 3.3 gather_fusion.3
  469.5 3.3 gather_fusion.3
  481.9 3.3 gather_fusion.3
  494.3 3.3 gather_fusion.3
  506.7 3.3 gather_fusion.3
  519.0 3.3 gather_fusion.3
  531.4 3.3 gather_fusion.3
  543.8 3.3 gather_fusion.3
  551.2 36.0 %reduce-scatter.3.cloned.1.call-done = f32[16,32,128]{2,1,0:T(8,128)} async-done(((f32[16,128,128]{2,1,0:T(8,128)}), f32[16,32,128]{2,1,0:T(8,128)}) %reduce-scatter.3.cloned.1.call-update) | async-done | bytes 262160 | tf_op jit(solution)/shard_map/reduce_scatter | solution.py:106
  588.2 28.2 %while.45 = (s32[]{:T(128)}, f32[8,64,256]{2,1,0:T(8,128)S(1)}, s32[8]{0:T(128)S(1)}, f32[16,32,128]{2,1,0:T(8,128)S(1)}, f32[16,128,256]{2,1,0:T(8,128)S(1)}, /...) while((s32[]{:T(128)}, f32[8,64,256]{2,1,0:T(8,128)S(1)}, s32[8]{0:T(128)S(1)}, ...), condition=%wide.region_10.11_spmd.clone, body=%wide.region_9.10_spmd.sunk.clone | while | flops 76857360 | bytes 713001 | solution.py:129
  617.8 724.9 %all-gather.2.cloned.1.call-done = f32[512,16384]{1,0:T(8,128)} async-done(((f32[8,16384]{1,0:T(8,128)}), f32[512,16384]{1,0:T(8,128)}) %all-gather.2.cloned.1.call-update) | async-done | bytes 33554448 | tf_op jit(solution)/shard_map/all_gather | solution.py:132
  1342.6 15.2 %fusion.130 = f32[8,16384]{1,0:T(8,128)S(1)} fusion(f32[512,16384]{1,0:T(8,128)} %all-gather.2.cloned.1.call-done, s32[8]{0:T(128)S(1)} %copy-done.9), kind=kOutput, calls=%fused_computation.186 | convolution fusion | flops 805310464 | bytes 34078752 | tf_op jit(solution)/shard_map/dot_general | solution.py:136
  1358.2 6.8 gather_fusion.6
  1365.2 2.1 fusion.123
  1367.2 1.8 fusion.122
  1369.5 55.7 %all-reduce.8.cloned.1.call-done = (f32[8,128,256]{2,1,0:T(8,128)}, f32[8,128,128]{2,1,0:T(8,128)}) async-done(((f32[8,128,256]{2,1,0:T(8,128)}, f32[8,128,128]{2,1,0:T(8,128)}), (f32[8,128,256]{2,1,0:T(8,128)}, f32[8,128,128]{2,1,0:T(8,128)})) %all-reduce.8.cloned.1.call-update) | async-done | bytes 1572880 | tf_op jit(solution)/shard_map/psum | solution.py:140
  1426.7 2.8 select_add_fusion.1
  1434.1 1.9 fusion.144
  1436.1 33.4 %reduce-scatter.5.cloned.1.call-done = f32[8,32,128]{2,1,0:T(8,128)} async-done(((f32[8,128,128]{2,1,0:T(8,128)}), f32[8,32,128]{2,1,0:T(8,128)}) %reduce-scatter.5.cloned.1.call-update) | async-done | bytes 131088 | tf_op jit(solution)/shard_map/reduce_scatter | solution.py:151
  (641 shorter events, 242.0 us)
Async XLA Ops:
  7.2 231.9 %all-reduce.10.cloned.1.call-start = ((), (), s32[]{:S(2)}) async-start(), calls=%async_computation.6 | async-start | bytes 6291456 | tf_op jit(solution)/shard_map/psum | solution.py:79
  8.1 7.4 collective-permute-start
  11.9 7.1 collective-permute-start.1
  154.7 1.0 copy-start.5
  154.7 86.0 %copy-start.8 = (s32[16,128]{1,0:T(8,128)S(1)}, s32[16,128]{1,0:T(8,128)}, u32[]{:S(2)}) copy-start(s32[16,128]{1,0:T(8,128)} %get-tuple-element.918) | copy-start | bytes 24580
  155.7 431.5 %reduce-scatter.3.cloned.1.call-start = ((), (), s32[]{:S(2)}) async-start(), calls=%async_computation.2 | async-start | bytes 1310720 | tf_op jit(solution)/shard_map/reduce_scatter | solution.py:106
  240.8 4.4 copy-start
  245.2 1.9 copy-start.2
  249.9 94.7 %collective-permute-start.2 = (f32[16,128,256]{2,1,0:T(8,128)S(1)}, f32[16,128,256]{2,1,0:T(8,128)}, u32[]{:S(2)}, u32[]{:S(2)}) collective-permute-start(f32[16,128,256]{2,1,0:T(8,128)S(1)} %multiply_add_fusion), channel_id=1, source_target_pairs={{0,4},{4,8},{8,12},{12,16},{16,20},{20,24},{24,28},{28,32},{32,36}... | collective-permute-start | bytes 6291464 | tf_op jit(solution)/shard_map/ppermute | solution.py:20
  254.2 92.2 %collective-permute-start.3 = (f32[16,128,256]{2,1,0:T(8,128)S(1)}, f32[16,128,256]{2,1,0:T(8,128)}, u32[]{:S(2)}, u32[]{:S(2)}) collective-permute-start(f32[16,128,256]{2,1,0:T(8,128)S(1)} %multiply_add_fusion), channel_id=1, source_target_pairs={{4,0},{8,4},{12,8},{16,12},{20,16},{24,20},{28,24},{32,28},{36,32}... | collective-permute-start | bytes 6291464 | tf_op jit(solution)/shard_map/ppermute | solution.py:22
  551.0 791.6 %all-gather.2.cloned.1.call-start = ((), (), s32[]{:S(2)}) async-start(), calls=%async_computation.3 | async-start | bytes 34078720 | tf_op jit(solution)/shard_map/all_gather | solution.py:132
  588.2 29.5 %copy-start.7 = (s32[8,128]{1,0:T(8,128)S(1)}, s32[8,128]{1,0:T(8,128)}, u32[]{:S(2)}) copy-start(s32[8,128]{1,0:T(8,128)} %param.19) | copy-start | bytes 12292
  588.2 29.5 %copy-start.10 = (s32[8]{0:T(128)S(1)}, s32[8]{0:T(128)}, u32[]{:S(2)}) copy-start(s32[8]{0:T(128)} %param.20) | copy-start | bytes 100
  588.2 754.4 %copy-start.9 = (s32[8]{0:T(128)S(1)}, s32[8]{0:T(128)}, u32[]{:S(2)}) copy-start(s32[8]{0:T(128)} %param.21) | copy-start | bytes 100
  616.5 741.3 %copy-start.6 = (f32[16,32,128]{2,1,0:T(8,128)}, f32[16,32,128]{2,1,0:T(8,128)S(1)}, u32[]{:S(2)}) copy-start(f32[16,32,128]{2,1,0:T(8,128)S(1)} %get-tuple-element.908) | copy-start | bytes 786436
  617.6 807.6 %all-reduce.8.cloned.1.call-start = ((), (), s32[]{:S(2)}) async-start(), calls=%async_computation.5 | async-start | bytes 3145728 | tf_op jit(solution)/shard_map/psum | solution.py:140
  1369.0 100.4 %reduce-scatter.5.cloned.1.call-start = ((), (), s32[]{:S(2)}) async-start(), calls=%async_computation.4 | async-start | bytes 655360 | tf_op jit(solution)/shard_map/reduce_scatter | solution.py:151
  1425.2 4.3 copy-start.1
  1425.2 4.3 copy-start.3
  1429.5 1.1 copy-start.4
Sparse Core Ops, SparseCore 0:
  155.8 83.1 all-reduce.9
  551.1 36.0 reduce-scatter.2
  617.7 724.8 all-gather.1
  1369.2 55.9 all-reduce.7
  1436.2 33.2 reduce-scatter.4
where the time goes:
time: 1480 us
  waiting for transfers between devices  1030 us (70%)
  local copies, waits for them, and re-layouts  169 us (11%)
  matrix products  143 us (10%)
  loops' own time  72.1 us (5%)
  other arithmetic  39 us (3%)
    all_gather x1, waiting for transfers between devices, local(): lax.all_gather(part, 'box', axis=0, tiled=True)  725 us
    ppermute x2, waiting for transfers between devices, with_halo(): lax.ppermute(tail, axis, [(i, (i + 1) % count) for i in range(ends)])  87.4 us
    psum x1, waiting for transfers between devices, local(): gram_part, right_part = lax.psum((gram_part, right_part), 'blk')  83.3 us
    psum x1, waiting for transfers between devices, local(): gram_two, right_two = lax.psum((gram_two, right_two), 'blk')  55.7 us
    gather x16, local copies, waits for them, and re-layouts, coarse(): near_fits = far_fits[near_cols]  53.6 us
    reduce_scatter x1, waiting for transfers between devices, local(): lax.psum_scatter(schur_term, 'blk', scatter_dimension=1, tiled=True)  36 us
    another operation x1, loops' own time, local(): block_rows, schur_term = lax.map(coarse, jnp.arange(box_count))  34.9 us
    reduce_scatter x1, waiting for transfers between devices, local(): lax.psum_scatter(parent_term, 'blk', scatter_dimension=1, tiled=True)  33.4 us
  transfers between devices with their start and end apart: 9, of which 8 were waited for; matrix products, arithmetic and copies ran while one was open for 0% of the time, Pallas kernels for 0%

commit v1 on v0

v1 whole, which is shorter than its diff:
```python
import functools

import jax
import jax.numpy as jnp
from jax import lax
from jax.experimental import pallas as pl
from jax.experimental.pallas import tpu as pltpu
from jax.sharding import PartitionSpec as P

STEPS = 3
MESH = pl.DeviceIdType.MESH
F32 = jnp.float32
BF16 = jnp.bfloat16
NN = (((1,), (0,)), ((), ()))
NT = (((1,), (1,)), ((), ()))
TN = (((0,), (0,)), ((), ()))
MIB = 1 << 20

HOMES, MEMBERS = 64, 4
BOXES, MINE = 16, 4
PANELS, SLOTS, NEAR = 256, 128, 8
UNITS = HOMES * 2
Z, W = 8, 8
PARENTS = 512
ROWS = SLOTS // MEMBERS


def halves(x):
    high = x.astype(BF16)
    return high, (x - high.astype(F32)).astype(BF16)


def dot(a, b, dims):
    return lax.dot_general(a, b, dims, preferred_element_type=F32)


def dot3(a, b, dims):
    return dot(a[0], b[0], dims) + (dot(a[0], b[1], dims) + dot(a[1], b[0], dims))


def square(a, dims):
    cross = dot(a[0], a[1], dims)
    return dot(a[0], a[0], dims) + (cross + cross.T)


def place():
    home, member = lax.axis_index("box"), lax.axis_index("blk")
    return home, member


def enter(peers):
    barrier = pltpu.get_barrier_semaphore()
    for peer in peers:
        pl.semaphore_signal(barrier, inc=1, device_id=peer, device_id_type=MESH)
    pl.semaphore_wait(barrier, len(peers))


def send(source, target, send_sem, recv_sem, peer):
    return pltpu.make_async_remote_copy(
        src_ref=source,
        dst_ref=target,
        send_sem=send_sem,
        recv_sem=recv_sem,
        device_id=peer,
        device_id_type=MESH,
    )


def halo_kernel(panels, window, own_sem, send_sem, recv_sem):
    home, member = place()
    after = (lax.rem(home + 1, HOMES), member)
    before = (lax.rem(home + HOMES - 1, HOMES), member)
    enter((after, before))
    up = send(panels, window.at[pl.ds(0, BOXES)], send_sem.at[0], recv_sem.at[0], after)
    down = send(panels, window.at[pl.ds(2 * BOXES, BOXES)], send_sem.at[1], recv_sem.at[1], before)
    own = pltpu.make_async_copy(panels, window.at[pl.ds(BOXES, BOXES)], own_sem)
    up.start()
    down.start()
    own.start()
    own.wait()
    up.wait()
    down.wait()


def halo(panels):
    return pl.pallas_call(
        halo_kernel,
        out_shape=jax.ShapeDtypeStruct((3 * BOXES, 4, PANELS), F32),
        in_specs=[pl.BlockSpec(memory_space=pl.ANY)],
        out_specs=pl.BlockSpec(memory_space=pl.ANY),
        scratch_shapes=[
            pltpu.SemaphoreType.DMA,
            pltpu.SemaphoreType.DMA((2,)),
            pltpu.SemaphoreType.DMA((2,)),
        ],
        compiler_params=pltpu.CompilerParams(collective_id=0, has_side_effects=True),
        name="halo",
    )(panels)


def refine(gram, right, chosen):
    steps = [1.0 / jnp.max(jnp.sum(jnp.abs(g), axis=1, keepdims=True), axis=0, keepdims=True) for g in gram]
    grams = [halves(g) for g in gram]
    fits = list(chosen)
    for _ in range(STEPS):
        updates = [r - dot3(g, halves(f), NN) for g, r, f in zip(grams, right, fits)]
        fits = [f + s * u for f, s, u in zip(fits, steps, updates)]
    return fits


def chosen_columns(row, count):
    position = lax.broadcasted_iota(jnp.int32, (2 * SLOTS, SLOTS), 0)
    slot = lax.broadcasted_iota(jnp.int32, (2 * SLOTS, SLOTS), 1)
    return jnp.where((position == row) & (slot < count), 1.0, 0.0).astype(F32)


def normal(square_matrix, columns):
    picks = columns.T
    picks16 = picks.astype(BF16)
    columns16 = columns.astype(BF16)
    high, low = halves(square_matrix)
    right = dot(picks16, high, NN) + dot(picks16, low, NN)
    high, low = halves(right)
    gram = dot(high, columns16, NN) + dot(low, columns16, NN)
    return gram, right, picks


def couple(col, row):
    total = None
    for axis in range(3):
        offset = col[axis] - row[axis]
        total = offset * offset if total is None else total + offset * offset
    return 0.03125 * lax.rsqrt(total + 0.01)


def fit_kernel(
    ids, near, count, window, skeleton, blocks, fitw_out, left_out, block_out, pair_out, column, high, low, sums
):
    home, member = ids[0], ids[1]
    base = (home - 1) * BOXES
    first = member * MINE
    tile = 64

    def fill(own, box, lane, write):
        for part in range(PANELS // SLOTS):
            lanes = slice(part * SLOTS, (part + 1) * SLOTS)
            row = [window[box, axis : axis + 1, lanes] for axis in range(3)]
            for start in range(0, PANELS, tile):
                col = [column[own, axis, start : start + tile, :] for axis in range(3)]
                hi, lo = halves(couple(col, row))
                write(start, part, hi, lo)

    for own in range(MINE):
        for axis in range(3):
            row = window[BOXES + first + own, axis : axis + 1, :]
            column[own, axis] = jnp.broadcast_to(row, (SLOTS, PANELS)).T

    def proxies(own, _):
        def one(index, _):
            box = near[first + own, index] - base

            def write(start, part, hi, lo):
                lanes = pl.ds(pl.multiple_of(index * PANELS + part * SLOTS, SLOTS), SLOTS)
                high[own, start : start + tile, lanes] = hi
                low[own, start : start + tile, lanes] = lo

            fill(own, box, None, write)
            return 0

        lax.fori_loop(0, NEAR, one, 0)
        sums[own] = square((high[own], low[own]), NT)
        return 0

    lax.fori_loop(0, MINE, proxies, 0)

    grams, rights, picks = [], [], []
    for own in range(MINE):
        columns = chosen_columns(skeleton[pl.ds(first + own, 1), :], count[first + own])
        gram, right, pick = normal(sums[own], columns)
        grams.append(gram)
        rights.append(right)
        picks.append(pick)
    fits = refine(grams, rights, picks)
    split = [halves(fit) for fit in fits]
    for own in range(MINE):
        self_term = window[BOXES + first + own, 3:4, :]
        weight = jnp.maximum(jnp.sum(fits[own] * fits[own] * self_term, axis=1, keepdims=True), 1.0)
        fitw_out[own] = fits[own] * lax.rsqrt(weight)
    for own in range(MINE):
        part = dot3(split[own], halves(blocks[own]), NN)
        block_out[own] = dot3(halves(part), split[own], NT)
    for own in range(MINE):
        for index in range(NEAR):
            lanes = slice(index * PANELS, (index + 1) * PANELS)
            left_out[own, :, lanes] = dot3(split[own], (high[own, :, lanes], low[own, :, lanes]), NN)
    for pair in range(MINE // 2):
        a, e = 2 * pair, 2 * pair + 1

        def write(start, part, hi, lo):
            lanes = slice(part * SLOTS, (part + 1) * SLOTS)
            high[a, start : start + tile, lanes] = hi
            low[a, start : start + tile, lanes] = lo

        fill(a, BOXES + first + e, None, write)
        part = dot3(split[a], (high[a, :, :PANELS], low[a, :, :PANELS]), NN)
        pair_out[pair] = dot3(halves(part), split[e], NT)


def whole(shape):
    return pl.BlockSpec(shape, lambda *_: (0,) * len(shape))


def fit_call(ids, near, count, window, skeleton, blocks):
    return pl.pallas_call(
        fit_kernel,
        grid_spec=pltpu.PrefetchScalarGridSpec(
            num_scalar_prefetch=3,
            grid=(1,),
            in_specs=[
                whole((3 * BOXES, 4, PANELS)),
                whole((BOXES, SLOTS)),
                pl.BlockSpec((MINE, PANELS, PANELS), lambda i, ids, *_: (ids[1], 0, 0)),
            ],
            out_specs=[
                whole((MINE, SLOTS, PANELS)),
                whole((MINE, SLOTS, NEAR * PANELS)),
                whole((MINE, SLOTS, SLOTS)),
                whole((MINE // 2, SLOTS, SLOTS)),
            ],
            scratch_shapes=[
                pltpu.VMEM((MINE, 3, PANELS, SLOTS), F32),
                pltpu.VMEM((MINE, PANELS, NEAR * PANELS), BF16),
                pltpu.VMEM((MINE, PANELS, NEAR * PANELS), BF16),
                pltpu.VMEM((MINE, PANELS, PANELS), F32),
            ],
        ),
        out_shape=[
            jax.ShapeDtypeStruct((MINE, SLOTS, PANELS), F32),
            jax.ShapeDtypeStruct((MINE, SLOTS, NEAR * PANELS), F32),
            jax.ShapeDtypeStruct((MINE, SLOTS, SLOTS), F32),
            jax.ShapeDtypeStruct((MINE // 2, SLOTS, SLOTS), F32),
        ],
        compiler_params=pltpu.CompilerParams(vmem_limit_bytes=56 * MIB),
        name="fit",
    )(ids, near, count, window, skeleton, blocks)


def exchange_kernel(fits, window, own_sem, send_sem, recv_sem, pass_sem, take_sem):
    home, member = place()
    side, core = member // 2, lax.rem(member, 2)
    unit = 2 * home + side

    def chip(shift):
        other = lax.rem(unit + shift + UNITS, UNITS)
        return (other // 2, 2 * lax.rem(other, 2) + core)

    sibling = (home, 2 * side + 1 - core)
    shifts = (1, -1, 2, -2)
    enter([sibling] + [chip(shift) for shift in shifts])

    def slot(shift):
        return window.at[2 * (2 + shift) + core]

    own = pltpu.make_async_copy(fits, slot(0), own_sem)
    sends = [
        send(fits, slot(-shift), send_sem.at[i], recv_sem.at[i], chip(shift)) for i, shift in enumerate(shifts)
    ]
    passes = [send(fits, slot(0), pass_sem.at[4], take_sem.at[4], sibling)] + [
        send(slot(-shift), slot(-shift), pass_sem.at[i], take_sem.at[i], sibling) for i, shift in enumerate(shifts)
    ]
    for copy in sends:
        copy.start()
    passes[0].start()
    own.start()
    for i in range(4):
        sends[i].wait_recv()
        passes[1 + i].start()
    own.wait()
    for copy in sends:
        copy.wait_send()
    for copy in passes:
        copy.wait()


def exchange(fits):
    return pl.pallas_call(
        exchange_kernel,
        out_shape=jax.ShapeDtypeStruct((10, MINE, SLOTS, PANELS), F32),
        in_specs=[pl.BlockSpec(memory_space=pl.ANY)],
        out_specs=pl.BlockSpec(memory_space=pl.ANY),
        scratch_shapes=[
            pltpu.SemaphoreType.DMA,
            pltpu.SemaphoreType.DMA((4,)),
            pltpu.SemaphoreType.DMA((4,)),
            pltpu.SemaphoreType.DMA((5,)),
            pltpu.SemaphoreType.DMA((5,)),
        ],
        compiler_params=pltpu.CompilerParams(collective_id=1, has_side_effects=True),
        name="exchange",
    )(fits)


def level_kernel(ids, near, count, fitw, left, block, pair, owners, skeleton, one_out, two_out, high, low, merged):
    home, member = ids[0], ids[1]
    first = member * MINE
    base = 16 * home + 8 * (member // 2) - 16

    for own in range(MINE):
        for index in range(NEAR):
            box = near[first + own, index] - base
            lanes = slice(index * PANELS, (index + 1) * PANELS)
            hi, lo = halves(dot3(halves(left[own, :, lanes]), halves(fitw[box]), NT))
            high[own, :, index * SLOTS : (index + 1) * SLOTS] = hi
            low[own, :, index * SLOTS : (index + 1) * SLOTS] = lo
        one_out[own] = block[own] - square((high[own], low[own]), NT)
    grams, rights, picks, bodies = [], [], [], []
    for j in range(MINE // 2):
        cross = pair[j]
        merged[j, :SLOTS, :SLOTS] = one_out[2 * j]
        merged[j, :SLOTS, SLOTS:] = cross
        merged[j, SLOTS:, :SLOTS] = cross.T
        merged[j, SLOTS:, SLOTS:] = one_out[2 * j + 1]
        body = halves(merged[j])
        parent = (home * BOXES + first) // 2 + j
        order = (
            lax.broadcasted_iota(jnp.int32, owners.shape, 0) * SLOTS
            + lax.broadcasted_iota(jnp.int32, owners.shape, 1)
        ).astype(F32)
        slot = jnp.sum(jnp.where(owners[...] == parent, order, 0.0)).astype(jnp.int32)
        columns = chosen_columns(skeleton[pl.ds(slot, 1), :], count[slot])
        gram, right, pick = normal(square(body, TN), columns)
        grams.append(gram)
        rights.append(right)
        picks.append(pick)
        bodies.append(body)
    fits = refine(grams, rights, picks)
    for j in range(MINE // 2):
        fit = halves(fits[j])
        two_out[j] = dot3(halves(dot3(fit, bodies[j], NN)), fit, NT)


def level_call(ids, near, count, fitw, left, block, pair, owners, skeleton):
    return pl.pallas_call(
        level_kernel,
        grid_spec=pltpu.PrefetchScalarGridSpec(
            num_scalar_prefetch=3,
            grid=(1,),
            in_specs=[
                whole(fitw.shape),
                whole(left.shape),
                whole(block.shape),
                whole(pair.shape),
                whole(owners.shape),
                whole(skeleton.shape),
            ],
            out_specs=[whole((MINE, SLOTS, SLOTS)), whole((MINE // 2, SLOTS, SLOTS))],
            scratch_shapes=[
                pltpu.VMEM((MINE, SLOTS, NEAR * SLOTS), BF16),
                pltpu.VMEM((MINE, SLOTS, NEAR * SLOTS), BF16),
                pltpu.VMEM((MINE // 2, PANELS, PANELS), F32),
            ],
        ),
        out_shape=[
            jax.ShapeDtypeStruct((MINE, SLOTS, SLOTS), F32),
            jax.ShapeDtypeStruct((MINE // 2, SLOTS, SLOTS), F32),
        ],
        compiler_params=pltpu.CompilerParams(vmem_limit_bytes=56 * MIB),
        name="level",
    )(ids, near, count, fitw, left, block, pair, owners, skeleton)


def route_kernel(
    owners, one, two, one_out, two_out, lines, packed, arrived,
    own_sem, row_send, row_recv, block_send, block_recv, line_send, line_recv, plane_send, plane_recv,
):
    home, member = place()
    across = 2 * (home // 16) + lax.rem(home, 2)
    along = lax.rem(home // 2, Z)

    def home_at(across_at, along_at):
        return (across_at // 2) * 16 + along_at * 2 + lax.rem(across_at, 2)

    members = [(home, lax.rem(member + d, MEMBERS)) for d in range(1, MEMBERS)]
    line = [(home_at(across, lax.rem(along + d, Z)), member) for d in range(1, Z)]
    plane_at = [lax.rem(across + d, W) for d in range(1, W)]
    plane = [(home_at(at, along), member) for at in plane_at]
    enter(members + line + plane)

    def rows(array, target):
        return array.at[:, pl.ds(pl.multiple_of(target * ROWS, ROWS), ROWS), :]

    ours = lines.at[along]
    own_two = pltpu.make_async_copy(rows(two, member), ours.at[pl.ds(2 * member, 2)], own_sem.at[0])
    own_one = pltpu.make_async_copy(rows(one, member), one_out.at[pl.ds(MINE * member, MINE)], own_sem.at[1])
    blocks = [
        send(rows(two, peer[1]), ours.at[pl.ds(2 * member, 2)], block_send.at[i], block_recv.at[i], peer)
        for i, peer in enumerate(members)
    ]
    ones = [
        send(rows(one, peer[1]), one_out.at[pl.ds(MINE * member, MINE)], row_send.at[i], row_recv.at[i], peer)
        for i, peer in enumerate(members)
    ]
    for copy in blocks:
        copy.start()
    own_two.start()
    own_one.start()
    for copy in ones:
        copy.start()
    own_two.wait()
    for copy in blocks:
        copy.wait_recv()
    gathers = [send(ours, ours, line_send.at[i], line_recv.at[i], peer) for i, peer in enumerate(line)]
    for copy in gathers:
        copy.start()
    for copy in gathers:
        copy.wait_recv()

    def pack(target, at):
        to = home_at(at, along)
        for s in range(8):
            parent = owners[8 * to + s]
            source = parent // 8
            target[s] = lines[lax.rem(source // 2, Z), lax.rem(parent, 8)]

    sends = []
    for i, peer in enumerate(plane):
        pack(packed.at[i], plane_at[i])
        copy = send(packed.at[i], arrived.at[across], plane_send.at[i], plane_recv.at[i], peer)
        copy.start()
        sends.append(copy)
    pack(arrived.at[across], across)
    for copy in sends:
        copy.wait_recv()
    for s in range(8):
        source = owners[8 * home + s] // 8
        two_out[s] = arrived[2 * (source // 16) + lax.rem(source, 2), s]
    own_one.wait()
    for copy in ones:
        copy.wait()
    for copy in blocks + gathers + sends:
        copy.wait_send()


def route(owners, one, two):
    dma = pltpu.SemaphoreType.DMA
    return pl.pallas_call(
        route_kernel,
        out_shape=[
            jax.ShapeDtypeStruct((BOXES, ROWS, SLOTS), F32),
            jax.ShapeDtypeStruct((8, ROWS, SLOTS), F32),
        ],
        in_specs=[
            pl.BlockSpec(memory_space=pltpu.SMEM),
            pl.BlockSpec(memory_space=pl.ANY),
            pl.BlockSpec(memory_space=pl.ANY),
        ],
        out_specs=[pl.BlockSpec(memory_space=pl.ANY), pl.BlockSpec(memory_space=pltpu.VMEM)],
        scratch_shapes=[
            pltpu.VMEM((Z, 8, ROWS, SLOTS), F32),
            pltpu.VMEM((W - 1, 8, ROWS, SLOTS), F32),
            pltpu.VMEM((W, 8, ROWS, SLOTS), F32),
            dma((2,)), dma((3,)), dma((3,)), dma((3,)), dma((3,)),
            dma((Z - 1,)), dma((Z - 1,)), dma((W - 1,)), dma((W - 1,)),
        ],
        compiler_params=pltpu.CompilerParams(collective_id=2, has_side_effects=True),
        name="route",
    )(owners, one, two)


def local(panels, self_blocks, neighbors, skeleton_one, count_one, skeleton_two, count_two, parent_at_slot):
    home, member = place()
    ids = jnp.stack([home, member]).astype(jnp.int32)
    owners = lax.all_gather(parent_at_slot, "box", axis=0, tiled=True)
    counts = lax.all_gather(count_two, "box", axis=0, tiled=True)
    skeletons = lax.all_gather(skeleton_two, "box", axis=0, tiled=True)
    window = halo(panels)
    fitw, left, block, pair = fit_call(ids, neighbors, count_one, window, skeleton_one, self_blocks)
    reach = exchange(fitw).reshape(10 * MINE, SLOTS, PANELS)
    one, two = level_call(
        ids, neighbors, counts, reach, left, block, pair, owners.reshape(4, SLOTS), skeletons
    )
    return route(owners, one, two)


def solution(mesh):
    placed = (
        P("box", None, None),
        P("box", None, None),
        P("box", None),
        P("box", None),
        P("box"),
        P("box", None),
        P("box"),
        P("box"),
    )
    return jax.shard_map(
        local,
        mesh=mesh,
        in_specs=placed,
        out_specs=(P("box", "blk", None), P("box", "blk", None)),
        check_vma=False,
    )
```

time: 1480 us -> 325 us (0.22)
  waiting for transfers between devices: 1030 us -> 0 us
  blocking collectives: 0 us -> 184 us
  local copies, waits for them, and re-layouts: 169 us -> 5.75 us
  matrix products: 143 us -> 0 us
  Pallas kernels: 0 us -> 127 us
  loops' own time: 72.1 us -> 0 us
  other arithmetic: 39 us -> 0.61 us
    all_gather x1 -> x0, waiting for transfers between devices: 725 us -> none  [local(): lax.all_gather(part, 'box', axis=0, tiled=True)]
    all_gather x0 -> x1, blocking collectives: none -> 163 us  [local(): skeletons = lax.all_gather(skeleton_two, 'box', axis=0, tiled=True)]
    dot_general x171 -> x0, matrix products: 143 us -> none  [the longest x17 26.8 us: normal_terms(): right_part = jnp.dot(picked_cols.T, proxy_kernel, precision=precise)]
    psum x2 -> x0, waiting for transfers between devices: 139 us -> none  [the longest x1 83.3 us: local(): gram_part, right_part = lax.psum((gram_part, right_part), 'blk')]
    pallas_call x0 -> x5, Pallas kernels: none -> 127 us  [the longest x1 44.7 us: route(): pl.pallas_call(route_kernel, out_shape=[jax.ShapeDtypeStruct((BOXES, ROWS...]
    gather x83 -> x0, local copies, waits for them, and re-layouts: 102 us -> none  [the longest x16 53.6 us: coarse(): near_fits = far_fits[near_cols]]
    ppermute x4 -> x0, waiting for transfers between devices: 91.9 us -> none  [the longest x2 87.4 us: with_halo(): lax.ppermute(tail, axis, [(i, (i + 1) % count) for i in range(ends)])]
    another operation x3 -> x0, loops' own time: 72.1 us -> none  [the longest x1 34.9 us: local(): block_rows, schur_term = lax.map(coarse, jnp.arange(box_count))]
  transfers between devices with their start and end apart: 9 -> 0, of which waited for: 8 -> 0; matrix products, arithmetic and copies ran while one was open for 0% -> 0% of each run, Pallas kernels for 0% -> 0%
where the time goes in v1:
time: 325 us; the launch traced here: 319 us
  blocking collectives  184 us (57%)
  Pallas kernels  127 us (39%)
  local copies, waits for them, and re-layouts  5.75 us (2%)
    all_gather x1, blocking collectives, local(): skeletons = lax.all_gather(skeleton_two, 'box', axis=0, tiled=True)  163 us
    pallas_call x1, Pallas kernels, route(): pl.pallas_call(route_kernel, out_shape=[jax.ShapeDtypeStruct((BOXES, ROWS...  44.7 us
    pallas_call x1, Pallas kernels, exchange(): pl.pallas_call(exchange_kernel, out_shape=jax.ShapeDtypeStruct((10, MINE,...  43.7 us
    unnamed x1, blocking collectives  20.8 us
    pallas_call x1, Pallas kernels, fit_call(): pl.pallas_call(fit_kernel, grid_spec=pltpu.PrefetchScalarGridSpec(num_sca...  16.6 us
    pallas_call x1, Pallas kernels, halo(): pl.pallas_call(halo_kernel, out_shape=jax.ShapeDtypeStruct((3 * BOXES, 4,...  12.4 us
    pallas_call x1, Pallas kernels, level_call(): pl.pallas_call(level_kernel, grid_spec=pltpu.PrefetchScalarGridSpec(num_s...  9.95 us

profile of v1, /device:TPU:2, one launch (start us, length us, event | category | flops | bytes accessed | tf_op | source)
XLA Modules:
  0.0 319.1 jit_solution(300478589643706480)
XLA Ops:
  0.6 0.6 pad_add_fusion.ids
  1.2 1.3 copy.11.near
  2.6 12.4 %halo.1.window = f32[48,4,256]{2,1,0:T(4,128)} custom-call(f32[16,4,256]{2,1,0:T(4,128)} %panels.1), custom_call_target="tpu_custom_call" | custom-call | tf_op jit(solution)/shard_map/halo/pallas_call | solution.py:86
  15.0 0.0 copy-start.3
  15.0 0.0 copy-start.1
  15.0 0.0 copy-start.2
  15.0 0.0 copy-start
  15.0 16.6 %fit.1 = (f32[4,128,256]{2,1,0:T(8,128)}, f32[4,128,2048]{2,1,0:T(8,128)}, f32[4,128,128]{2,1,0:T(8,128)}, f32[2,128,128]{2,1,0:T(8,128)}) custom-call(s32[2]{0:T(128)} %pad_add_fusion.ids, s32[16,8]{1,0:T(8,128)} %copy.11.near, s32[16]{0:T(128)} %count.1, f32[48,4,256]{2,1,0:T(4,128)} %halo.1.window, s32[16,128]{1,0:T(8,128)} %skeleton.1, ...), custom_call_target="tpu_custom_call" | custom-call | tf_op jit(solution)/shard_map/fit/pallas_call | solution.py:214
  31.7 43.7 %exchange.1 = f32[10,4,128,256]{3,2,1,0:T(8,128)} custom-call(f32[4,128,256]{2,1,0:T(8,128)} %get-tuple-element.8.fits), custom_call_target="tpu_custom_call" | custom-call | tf_op jit(solution)/shard_map/exchange/pallas_call | solution.py:286
  75.3 0.0 copy-done.3
  75.4 0.7 dynamic-slice
  76.7 0.0 copy-done.1
  76.7 0.2 dynamic-update-slice
  77.0 0.0 copy-done.2
  77.0 0.2 dynamic-update-slice.1
  77.2 20.8 %all-reduce.2 = (s32[512]{0:T(512)}, s32[512]{0:T(512)}) all-reduce(s32[512]{0:T(512)S(1)} %dynamic-update-slice, s32[512]{0:T(512)S(1)} %dynamic-update-slice.1), channel_id=1, replica_groups=mesh['box'=64,'blk'=4] {'box'}, use_global_device_ids=true, to_apply=%add | all-reduce | flops 1024 | bytes 8192
  98.0 0.0 copy-done
  98.0 163.2 %all_gather.11.skeleton = s32[512,128]{1,0:T(8,128)} all-gather(s32[8,128]{1,0:T(8,128)S(1)} %copy-done), channel_id=1, replica_groups=mesh['box'=64,'blk'=4] {'box'}, dimensions={0}, use_global_device_ids=true | all-gather | bytes 266240 | tf_op jit(solution)/shard_map/all_gather | solution.py:475
  261.2 9.9 %level.1 = (f32[4,128,128]{2,1,0:T(8,128)}, f32[2,128,128]{2,1,0:T(8,128)}) custom-call(s32[2]{0:T(128)} %pad_add_fusion.ids, s32[16,8]{1,0:T(8,128)} %copy.11.near, s32[512]{0:T(512)} %get-tuple-element.15.count, f32[40,128,256]{2,1,0:T(8,128)} %bitcast.5, f32[4,128,2048]{2,1,0:T(8,128)} %get-tuple-element.9.left, f32[4,128,128]{2,1,0:T(8,128)} %get-tuple-element.10.block, ...), custom_call_target="tpu_custom_call" | custom-call | tf_op jit(solution)/shard_map/level/pallas_call | solution.py:343
  271.1 44.7 %route.1 = (f32[16,32,128]{2,1,0:T(8,128)}, f32[8,32,128]{2,1,0:T(8,128)}) custom-call(s32[512]{0:T(512)} %get-tuple-element.14.owners, f32[4,128,128]{2,1,0:T(8,128)} %get-tuple-element.12.one, f32[2,128,128]{2,1,0:T(8,128)} %get-tuple-element.13.two), custom_call_target="tpu_custom_call" | custom-call | tf_op jit(solution)/shard_map/route/pallas_call | solution.py:446
  315.9 1.7 copy.16
  317.6 1.6 copy.17
  (2 shorter events, 0.0 us)
Async XLA Ops:
  15.0 60.4 %copy-start.3 = (u32[256]{0:T(256)S(1)}, u32[256]{0:T(256)}, u32[]{:S(2)}) copy-start(u32[256]{0:T(256)} %constant.19) | copy-start | bytes 3076
  15.0 61.7 %copy-start.1 = (s32[8]{0:T(128)S(1)}, s32[8]{0:T(128)}, u32[]{:S(2)}) copy-start(s32[8]{0:T(128)} %param.15) | copy-start | bytes 100
  15.0 62.0 %copy-start.2 = (s32[8]{0:T(128)S(1)}, s32[8]{0:T(128)}, u32[]{:S(2)}) copy-start(s32[8]{0:T(128)} %param.14) | copy-start | bytes 100
  15.0 83.0 %copy-start = (s32[8,128]{1,0:T(8,128)S(1)}, s32[8,128]{1,0:T(8,128)}, u32[]{:S(2)}) copy-start(s32[8,128]{1,0:T(8,128)} %param.13) | copy-start | bytes 12292

commit v2 on v1

--- a/solution.py
+++ b/solution.py
@@ -23,6 +23,7 @@
 Z, W = 8, 8
 PARENTS = 512
 ROWS = SLOTS // MEMBERS
+PARTS = 2
 
 
 def halves(x):
@@ -64,6 +65,19 @@
         device_id=peer,
         device_id_type=MESH,
     )
+
+
+def home_at(across, along):
+    return (across // 2) * 16 + along * 2 + lax.rem(across, 2)
+
+
+def lines_of(home, member):
+    across = 2 * (home // 16) + lax.rem(home, 2)
+    along = lax.rem(home // 2, Z)
+    line = [(home_at(across, lax.rem(along + d, Z)), member) for d in range(1, Z)]
+    spots = [lax.rem(across + d, W) for d in range(1, W)]
+    plane = [(spot, (home_at(spot, along), member)) for spot in spots]
+    return line, plane, across, along
 
 
 def halo_kernel(panels, window, own_sem, send_sem, recv_sem):
@@ -245,62 +259,182 @@
     )(ids, near, count, window, skeleton, blocks)
 
 
-def exchange_kernel(fits, window, own_sem, send_sem, recv_sem, pass_sem, take_sem):
+def exchange_kernel(
+    skeleton, owners, counts, fits, window, table,
+    mine, via, own_sem, send_sem, recv_sem, pass_sem, take_sem, line_send, line_recv, plane_send, plane_recv,
+):
     home, member = place()
-    side, core = member // 2, lax.rem(member, 2)
-    unit = 2 * home + side
-
-    def chip(shift):
-        other = lax.rem(unit + shift + UNITS, UNITS)
-        return (other // 2, 2 * lax.rem(other, 2) + core)
-
-    sibling = (home, 2 * side + 1 - core)
-    shifts = (1, -1, 2, -2)
-    enter([sibling] + [chip(shift) for shift in shifts])
-
-    def slot(shift):
-        return window.at[2 * (2 + shift) + core]
-
-    own = pltpu.make_async_copy(fits, slot(0), own_sem)
-    sends = [
-        send(fits, slot(-shift), send_sem.at[i], recv_sem.at[i], chip(shift)) for i, shift in enumerate(shifts)
-    ]
-    passes = [send(fits, slot(0), pass_sem.at[4], take_sem.at[4], sibling)] + [
-        send(slot(-shift), slot(-shift), pass_sem.at[i], take_sem.at[i], sibling) for i, shift in enumerate(shifts)
-    ]
-    for copy in sends:
-        copy.start()
-    passes[0].start()
-    own.start()
-    for i in range(4):
-        sends[i].wait_recv()
-        passes[1 + i].start()
-    own.wait()
-    for copy in sends:
-        copy.wait_send()
-    for copy in passes:
-        copy.wait()
-
-
-def exchange(fits):
+    side_hi, core = member // 2, lax.rem(member, 2)
+    side_lo = lax.rem(home, 2)
+    sign = 1 - 2 * side_hi
+    outer = side_lo == side_hi
+    flipped = home + 1 - 2 * side_lo
+    side = (flipped, member)
+    cross = (flipped, 2 * (1 - side_hi) + core)
+    above = (lax.rem(home + 2 * sign + HOMES, HOMES), member)
+    below = (lax.rem(home - 2 * sign + HOMES, HOMES), member)
+    sibling = (home, 2 * side_hi + 1 - core)
+    line, plane, across, along = lines_of(home, member)
+    enter([side, cross, above, below, sibling] + line + [peer for _, peer in plane])
+
+    def slot(shift, k, to=1):
+        return window.at[2 * (2 + to * sign * shift) + core, k]
+
+    def moved(source, target, stream, k, peer, recv):
+        return send(source, target, send_sem.at[stream, k], recv_sem.at[recv, k], peer)
+
+    def passed(source, shift, i, k):
+        return send(source, slot(shift, k), pass_sem.at[i, k], take_sem.at[i, k], sibling)
+
+    boxes = range(MINE)
+    own = pltpu.make_async_copy(fits, window.at[4 + core], own_sem.at[0])
+
+    lane = lax.broadcasted_iota(jnp.int32, (1, SLOTS), 1)
+    owner_row = jnp.zeros((1, SLOTS), jnp.int32)
+    count_row = jnp.zeros((1, SLOTS), jnp.int32)
+    for s in range(8):
+        owner_row = jnp.where(lane == s, owners[s], owner_row)
+        count_row = jnp.where(lane == s, counts[s], count_row)
+    mine[0:8, :] = skeleton[...]
+    mine[8:16, :] = jnp.zeros((8, SLOTS), jnp.int32)
+    mine[8:9, :] = owner_row
+    mine[9:10, :] = count_row
+
+    def own_streams(first_peer, first_target, second_peer, second_target, second_recv):
+        copies = []
+        for k in boxes:
+            copies.append(moved(fits.at[k], first_target(k), 0, k, first_peer, 0))
+            copies.append(moved(fits.at[k], second_target(k), 1, k, second_peer, second_recv))
+            copies.append(passed(fits.at[k], 0, 4, k))
+        for copy in copies:
+            copy.start()
+        own.start()
+        return copies
+
+    def arrival(shift, stream, k):
+        return moved(slot(shift, k), slot(shift, k), stream, k, side, stream)
+
+    def gather_line():
+        spot = table.at[across, along]
+        placed = pltpu.make_async_copy(mine, spot, own_sem.at[1])
+        placed.start()
+        copies = [send(mine, spot, line_send.at[i], line_recv.at[i], peer) for i, peer in enumerate(line)]
+        for copy in copies:
+            copy.start()
+        placed.wait()
+        return copies
+
+    def gather_plane():
+        copies = [
+            send(table.at[across], table.at[across], plane_send.at[i], plane_recv.at[i], peer)
+            for i, (_, peer) in enumerate(plane)
+        ]
+        for copy in copies:
+            copy.start()
+        return copies
+
+    def finish(copies, gathers):
+        for copy in copies + gathers:
+            copy.wait_send()
+        for i in range(5):
+            for k in boxes:
+                passed(fits.at[k], 0, i, k).wait_recv()
+        own.wait()
+
+    def start(copies, *new):
+        for copy in new:
+            copy.start()
+            copies.append(copy)
+
+    @pl.when(outer)
+    def _():
+        copies = own_streams(
+            side, lambda k: slot(-2, k), below, lambda k: via.at[k], 1
+        )
+        gathers = gather_line()
+        planes = []
+        for k in range(MINE + 1):
+            if k < MINE:
+                arrival(2, 0, k).wait_recv()
+                start(copies, moved(slot(2, k), slot(-2, k), 2, k, above, 2))
+                if k % 2:
+                    start(copies, moved(slot(2, k), slot(1, k, -1), 4, k, cross, 4))
+                start(copies, passed(slot(2, k), 2, 0, k))
+                moved(via.at[k], via.at[k], 1, k, side, 1).wait_recv()
+                start(copies, moved(via.at[k], slot(-1, k, -1), 3, k, cross, 3))
+            if k == 1:
+                for copy in gathers:
+                    copy.wait_recv()
+                planes = gather_plane()
+            if k:
+                arrival(-2, 2, k - 1).wait_recv()
+                start(copies, passed(slot(-2, k - 1), -2, 1, k - 1))
+                arrival(-1, 3, k - 1).wait_recv()
+                start(copies, passed(slot(-1, k - 1), -1, 2, k - 1))
+                arrival(1, 4, k - 1).wait_recv()
+                start(copies, passed(slot(1, k - 1), 1, 3, k - 1))
+        for copy in planes:
+            copy.wait_recv()
+        finish(copies, gathers + planes)
+
+    @pl.when(jnp.logical_not(outer))
+    def _():
+        copies = own_streams(
+            side, lambda k: slot(2, k), cross, lambda k: slot(-1, k, -1), 1
+        )
+        gathers = gather_line()
+        planes = []
+        for k in range(MINE + 1):
+            if k < MINE:
+                arrival(-2, 0, k).wait_recv()
+                start(copies, moved(slot(-2, k), slot(1, k, -1), 2, k, cross, 2))
+                start(copies, moved(slot(-2, k), slot(2, k), 3, k, below, 3))
+                start(copies, passed(slot(-2, k), -2, 0, k))
+                arrival(-1, 1, k).wait_recv()
+                if k % 2 == 0:
+                    start(copies, moved(slot(-1, k), slot(1, k), 4, k, side, 4))
+                start(copies, passed(slot(-1, k), -1, 1, k))
+            if k == 1:
+                for copy in gathers:
+                    copy.wait_recv()
+                planes = gather_plane()
+            if k:
+                arrival(1, 2, k - 1).wait_recv()
+                start(copies, passed(slot(1, k - 1), 1, 2, k - 1))
+                arrival(2, 3, k - 1).wait_recv()
+                start(copies, passed(slot(2, k - 1), 2, 3, k - 1))
+        for copy in planes:
+            copy.wait_recv()
+        finish(copies, gathers + planes)
+
+
+def exchange(skeleton, owners, counts, fits):
+    dma = pltpu.SemaphoreType.DMA
     return pl.pallas_call(
         exchange_kernel,
-        out_shape=jax.ShapeDtypeStruct((10, MINE, SLOTS, PANELS), F32),
-        in_specs=[pl.BlockSpec(memory_space=pl.ANY)],
-        out_specs=pl.BlockSpec(memory_space=pl.ANY),
+        out_shape=[
+            jax.ShapeDtypeStruct((10, MINE, SLOTS, PANELS), F32),
+            jax.ShapeDtypeStruct((W, Z, 16, SLOTS), jnp.int32),
+        ],
+        in_specs=[
+            pl.BlockSpec(memory_space=pltpu.VMEM),
+            pl.BlockSpec(memory_space=pltpu.SMEM),
+            pl.BlockSpec(memory_space=pltpu.SMEM),
+            pl.BlockSpec(memory_space=pl.ANY),
+        ],
+        out_specs=[pl.BlockSpec(memory_space=pl.ANY)] * 2,
         scratch_shapes=[
-            pltpu.SemaphoreType.DMA,
-            pltpu.SemaphoreType.DMA((4,)),
-            pltpu.SemaphoreType.DMA((4,)),
-            pltpu.SemaphoreType.DMA((5,)),
-            pltpu.SemaphoreType.DMA((5,)),
+            pltpu.VMEM((16, SLOTS), jnp.int32),
+            pltpu.VMEM((MINE, SLOTS, PANELS), F32),
+            dma((2,)), dma((5, MINE)), dma((5, MINE)), dma((5, MINE)), dma((5, MINE)),
+            dma((Z - 1,)), dma((Z - 1,)), dma((W - 1,)), dma((W - 1,)),
         ],
         compiler_params=pltpu.CompilerParams(collective_id=1, has_side_effects=True),
         name="exchange",
-    )(fits)
-
-
-def level_kernel(ids, near, count, fitw, left, block, pair, owners, skeleton, one_out, two_out, high, low, merged):
+    )(skeleton, owners, counts, fits)
+
+
+def level_kernel(ids, near, fitw, left, block, pair, table, one_out, two_out, high, low, merged):
     home, member = ids[0], ids[1]
     first = member * MINE
     base = 16 * home + 8 * (member // 2) - 16
@@ -322,12 +456,14 @@
         merged[j, SLOTS:, SLOTS:] = one_out[2 * j + 1]
         body = halves(merged[j])
         parent = (home * BOXES + first) // 2 + j
-        order = (
-            lax.broadcasted_iota(jnp.int32, owners.shape, 0) * SLOTS
-            + lax.broadcasted_iota(jnp.int32, owners.shape, 1)
-        ).astype(F32)
-        slot = jnp.sum(jnp.where(owners[...] == parent, order, 0.0)).astype(jnp.int32)
-        columns = chosen_columns(skeleton[pl.ds(slot, 1), :], count[slot])
+        spot = lax.broadcasted_iota(jnp.int32, (W * Z, SLOTS), 0)
+        lane = lax.broadcasted_iota(jnp.int32, (W * Z, SLOTS), 1)
+        found = (table[:, 8, :] == parent) & (lane < 8)
+        slot = jnp.sum(jnp.where(found, (8 * spot + lane).astype(F32), 0.0)).astype(jnp.int32)
+        spot, slot = slot // 8, lax.rem(slot, 8)
+        lane = lax.broadcasted_iota(jnp.int32, (1, SLOTS), 1)
+        count = jnp.sum(jnp.where(lane == slot, table[spot, 9:10, :].astype(F32), 0.0)).astype(jnp.int32)
+        columns = chosen_columns(table[spot, pl.ds(slot, 1), :], count)
         gram, right, pick = normal(square(body, TN), columns)
         grams.append(gram)
         rights.append(right)
@@ -339,19 +475,18 @@
         two_out[j] = dot3(halves(dot3(fit, bodies[j], NN)), fit, NT)
 
 
-def level_call(ids, near, count, fitw, left, block, pair, owners, skeleton):
+def level_call(ids, near, fitw, left, block, pair, table):
     return pl.pallas_call(
         level_kernel,
         grid_spec=pltpu.PrefetchScalarGridSpec(
-            num_scalar_prefetch=3,
+            num_scalar_prefetch=2,
             grid=(1,),
             in_specs=[
                 whole(fitw.shape),
                 whole(left.shape),
                 whole(block.shape),
                 whole(pair.shape),
-                whole(owners.shape),
-                whole(skeleton.shape),
+                whole(table.shape),
             ],
             out_specs=[whole((MINE, SLOTS, SLOTS)), whole((MINE // 2, SLOTS, SLOTS))],
             scratch_shapes=[
@@ -366,120 +501,167 @@
         ],
         compiler_params=pltpu.CompilerParams(vmem_limit_bytes=56 * MIB),
         name="level",
-    )(ids, near, count, fitw, left, block, pair, owners, skeleton)
+    )(ids, near, fitw, left, block, pair, table)
 
 
 def route_kernel(
-    owners, one, two, one_out, two_out, lines, packed, arrived,
-    own_sem, row_send, row_recv, block_send, block_recv, line_send, line_recv, plane_send, plane_recv,
+    table, one, two, one_out, two_out, owners, lines0, lines1, packed, arrived0, arrived1,
+    own_sem, row_send, row_recv, block_send, block_recv, up_send, up_recv, down_send, down_recv, plane_send, plane_recv,
 ):
     home, member = place()
-    across = 2 * (home // 16) + lax.rem(home, 2)
-    along = lax.rem(home // 2, Z)
-
-    def home_at(across_at, along_at):
-        return (across_at // 2) * 16 + along_at * 2 + lax.rem(across_at, 2)
-
+    line, plane, across, along = lines_of(home, member)
+    up, down = line[0], line[-1]
     members = [(home, lax.rem(member + d, MEMBERS)) for d in range(1, MEMBERS)]
-    line = [(home_at(across, lax.rem(along + d, Z)), member) for d in range(1, Z)]
-    plane_at = [lax.rem(across + d, W) for d in range(1, W)]
-    plane = [(home_at(at, along), member) for at in plane_at]
-    enter(members + line + plane)
-
-    def rows(array, target):
-        return array.at[:, pl.ds(pl.multiple_of(target * ROWS, ROWS), ROWS), :]
-
-    ours = lines.at[along]
-    own_two = pltpu.make_async_copy(rows(two, member), ours.at[pl.ds(2 * member, 2)], own_sem.at[0])
-    own_one = pltpu.make_async_copy(rows(one, member), one_out.at[pl.ds(MINE * member, MINE)], own_sem.at[1])
+    listing = pltpu.make_async_copy(table.at[:, 8], owners, own_sem.at[2])
+    listing.start()
+    enter(members + [up, down] + [peer for _, peer in plane])
+    half = ROWS // PARTS
+    lines, arrived = (lines0, lines1), (arrived0, arrived1)
+
+    def rows(array, target, part=None):
+        first, count = (target * ROWS, ROWS) if part is None else (target * ROWS + part * half, half)
+        return array.at[:, pl.ds(pl.multiple_of(first, half), count), :]
+
+    def ours(part):
+        return lines[part].at[along, pl.ds(2 * member, 2)]
+
+    own_two = [
+        pltpu.make_async_copy(rows(two, member, part), ours(part), own_sem.at[3 + part]) for part in range(PARTS)
+    ]
+    own_one = pltpu.make_async_copy(rows(one, member), one_out.at[pl.ds(MINE * member, MINE)], own_sem.at[0])
     blocks = [
-        send(rows(two, peer[1]), ours.at[pl.ds(2 * member, 2)], block_send.at[i], block_recv.at[i], peer)
-        for i, peer in enumerate(members)
+        [
+            send(rows(two, peer[1], part), ours(part), block_send.at[part, i], block_recv.at[part, i], peer)
+            for i, peer in enumerate(members)
+        ]
+        for part in range(PARTS)
     ]
     ones = [
         send(rows(one, peer[1]), one_out.at[pl.ds(MINE * member, MINE)], row_send.at[i], row_recv.at[i], peer)
         for i, peer in enumerate(members)
     ]
-    for copy in blocks:
-        copy.start()
-    own_two.start()
-    own_one.start()
+    for part in range(PARTS):
+        for copy in blocks[part]:
+            copy.start()
+        own_two[part].start()
     for copy in ones:
         copy.start()
-    own_two.wait()
-    for copy in blocks:
-        copy.wait_recv()
-    gathers = [send(ours, ours, line_send.at[i], line_recv.at[i], peer) for i, peer in enumerate(line)]
-    for copy in gathers:
-        copy.start()
-    for copy in gathers:
-        copy.wait_recv()
+    own_one.start()
+
+    def upward(part, step):
+        spot = lines[part].at[lax.rem(along - step + Z, Z)]
+        return send(spot, spot, up_send.at[part, step], up_recv.at[part, step], up)
+
+    def downward(part, step):
+        spot = lines[part].at[lax.rem(along + step, Z)]
+        return send(spot, spot, down_send.at[part, step], down_recv.at[part, step], down)
+
+    def steps(part):
+        return (4, 3) if part % 2 == 0 else (3, 4)
+
+    def gather(part, step):
+        for way, copy in enumerate((upward, downward)):
+            if step and step - 1 < steps(part)[way]:
+                copy(part, step - 1).wait_recv()
+            if step < steps(part)[way]:
+                copy(part, step).start()
 
     def pack(target, at):
-        to = home_at(at, along)
+        spot = 8 * at + along
         for s in range(8):
-            parent = owners[8 * to + s]
+            parent = owners[spot, s]
             source = parent // 8
-            target[s] = lines[lax.rem(source // 2, Z), lax.rem(parent, 8)]
-
-    sends = []
-    for i, peer in enumerate(plane):
-        pack(packed.at[i], plane_at[i])
-        copy = send(packed.at[i], arrived.at[across], plane_send.at[i], plane_recv.at[i], peer)
-        copy.start()
-        sends.append(copy)
-    pack(arrived.at[across], across)
-    for copy in sends:
-        copy.wait_recv()
-    for s in range(8):
-        source = owners[8 * home + s] // 8
-        two_out[s] = arrived[2 * (source // 16) + lax.rem(source, 2), s]
+            target(s, lax.rem(source // 2, Z), lax.rem(parent, 8))
+
+    def across_copy(part, i):
+        return send(
+            packed.at[part, i], arrived[part].at[across], plane_send.at[part, i], plane_recv.at[part, i], plane[i][1]
+        )
+
+    def send_across(part):
+        for i, (spot, _) in enumerate(plane):
+
+            def put(s, z, j):
+                packed[part, i, s] = lines[part][z, j]
+
+            pack(put, spot)
+            across_copy(part, i).start()
+
+        def put(s, z, j):
+            arrived[part][across, s] = lines[part][z, j]
+
+        pack(put, across)
+
+    for part in range(PARTS):
+        own_two[part].wait()
+        for copy in blocks[part]:
+            copy.wait_recv()
+        gather(part, 0)
+    listing.wait()
+    for step in range(1, 6):
+        if step < 5:
+            gather(0, step)
+        if step > 1:
+            gather(1, step - 1)
+        if step > 3:
+            send_across(step - 4)
+    spot = 8 * across + along
+    for part in range(PARTS):
+        for i in range(W - 1):
+            across_copy(part, i).wait_recv()
+        for s in range(8):
+            source = owners[spot, s] // 8
+            two_out[s, part * half : (part + 1) * half, :] = arrived[part][2 * (source // 16) + lax.rem(source, 2), s]
     own_one.wait()
     for copy in ones:
         copy.wait()
-    for copy in blocks + gathers + sends:
-        copy.wait_send()
-
-
-def route(owners, one, two):
+    for part in range(PARTS):
+        for copy in blocks[part]:
+            copy.wait_send()
+        for step in range(4):
+            for way, copy in enumerate((upward, downward)):
+                if step < steps(part)[way]:
+                    copy(part, step).wait_send()
+        for i in range(W - 1):
+            across_copy(part, i).wait_send()
+
+
+def route(table, one, two):
     dma = pltpu.SemaphoreType.DMA
+    half = ROWS // PARTS
     return pl.pallas_call(
         route_kernel,
         out_shape=[
             jax.ShapeDtypeStruct((BOXES, ROWS, SLOTS), F32),
             jax.ShapeDtypeStruct((8, ROWS, SLOTS), F32),
         ],
-        in_specs=[
-            pl.BlockSpec(memory_space=pltpu.SMEM),
-            pl.BlockSpec(memory_space=pl.ANY),
-            pl.BlockSpec(memory_space=pl.ANY),
-        ],
+        in_specs=[pl.BlockSpec(memory_space=pl.ANY)] * 3,
         out_specs=[pl.BlockSpec(memory_space=pl.ANY), pl.BlockSpec(memory_space=pltpu.VMEM)],
         scratch_shapes=[
-            pltpu.VMEM((Z, 8, ROWS, SLOTS), F32),
-            pltpu.VMEM((W - 1, 8, ROWS, SLOTS), F32),
-            pltpu.VMEM((W, 8, ROWS, SLOTS), F32),
-            dma((2,)), dma((3,)), dma((3,)), dma((3,)), dma((3,)),
-            dma((Z - 1,)), dma((Z - 1,)), dma((W - 1,)), dma((W - 1,)),
+            pltpu.SMEM((W * Z, SLOTS), jnp.int32),
+            pltpu.VMEM((Z, 8, half, SLOTS), F32),
+            pltpu.VMEM((Z, 8, half, SLOTS), F32),
+            pltpu.VMEM((PARTS, W - 1, 8, half, SLOTS), F32),
+            pltpu.VMEM((W, 8, half, SLOTS), F32),
+            pltpu.VMEM((W, 8, half, SLOTS), F32),
+            dma((3 + PARTS,)), dma((3,)), dma((3,)), dma((PARTS, 3)), dma((PARTS, 3)),
+            dma((PARTS, 4)), dma((PARTS, 4)), dma((PARTS, 4)), dma((PARTS, 4)),
+            dma((PARTS, W - 1)), dma((PARTS, W - 1)),
         ],
         compiler_params=pltpu.CompilerParams(collective_id=2, has_side_effects=True),
         name="route",
-    )(owners, one, two)
+    )(table, one, two)
 
 
 def local(panels, self_blocks, neighbors, skeleton_one, count_one, skeleton_two, count_two, parent_at_slot):
     home, member = place()
     ids = jnp.stack([home, member]).astype(jnp.int32)
-    owners = lax.all_gather(parent_at_slot, "box", axis=0, tiled=True)
-    counts = lax.all_gather(count_two, "box", axis=0, tiled=True)
-    skeletons = lax.all_gather(skeleton_two, "box", axis=0, tiled=True)
     window = halo(panels)
     fitw, left, block, pair = fit_call(ids, neighbors, count_one, window, skeleton_one, self_blocks)
-    reach = exchange(fitw).reshape(10 * MINE, SLOTS, PANELS)
-    one, two = level_call(
-        ids, neighbors, counts, reach, left, block, pair, owners.reshape(4, SLOTS), skeletons
-    )
-    return route(owners, one, two)
+    reach, table = exchange(skeleton_two, parent_at_slot, count_two, fitw)
+    reach, table = reach.reshape(10 * MINE, SLOTS, PANELS), table.reshape(W * Z, 16, SLOTS)
+    one, two = level_call(ids, neighbors, reach, left, block, pair, table)
+    return route(table, one, two)
 
 
 def solution(mesh):

time: 325 us -> 113 us (0.35); the launches traced: 319 us -> 113 us
  blocking collectives: 184 us -> 0 us
  Pallas kernels: 127 us -> 107 us
    all_gather x1 -> x0, blocking collectives: 163 us -> none  [local(): skeletons = lax.all_gather(skeleton_two, 'box', axis=0, tiled=True)]
    unnamed x1 -> x0, blocking collectives: 20.8 us -> none
    pallas_call x1, Pallas kernels: 43.7 us -> 32.6 us  [exchange(): pl.pallas_call(exchange_kernel, out_shape=[jax.ShapeDtypeStruct((10, MINE...]
    pallas_call x1, Pallas kernels: 44.7 us -> 35.7 us  [route(): pl.pallas_call(route_kernel, out_shape=[jax.ShapeDtypeStruct((BOXES, ROWS...]
where the time goes in v2:
time: 113 us
  Pallas kernels  107 us (95%)
  local copies, waits for them, and re-layouts  4.59 us (4%)
    pallas_call x1, Pallas kernels, route(): pl.pallas_call(route_kernel, out_shape=[jax.ShapeDtypeStruct((BOXES, ROWS...  35.7 us
    pallas_call x1, Pallas kernels, exchange(): pl.pallas_call(exchange_kernel, out_shape=[jax.ShapeDtypeStruct((10, MINE...  32.6 us
    pallas_call x1, Pallas kernels, fit_call(): pl.pallas_call(fit_kernel, grid_spec=pltpu.PrefetchScalarGridSpec(num_sca...  16.5 us
    pallas_call x1, Pallas kernels, halo(): pl.pallas_call(halo_kernel, out_shape=jax.ShapeDtypeStruct((3 * BOXES, 4,...  12.4 us
    pallas_call x1, Pallas kernels, level_call(): pl.pallas_call(level_kernel, grid_spec=pltpu.PrefetchScalarGridSpec(num_s...  10 us
    unnamed x3, local copies, waits for them, and re-layouts  4.59 us

profile of v2, /device:TPU:2, one launch (start us, length us, event | category | flops | bytes accessed | tf_op | source)
XLA Modules:
  0.0 113.0 jit_solution(8214834644194333544)
XLA Ops:
  0.6 0.6 pad_add_fusion.ids
  1.2 1.4 %copy.10.near = s32[16,8]{1,0:T(8,128)} copy(s32[16,8]{0,1:T(8,128)} %param.10) | data formatting | bytes 1024 | tf_op args[2]
  2.6 12.4 %halo.1.window = f32[48,4,256]{2,1,0:T(4,128)} custom-call(f32[16,4,256]{2,1,0:T(4,128)} %panels.1), custom_call_target="tpu_custom_call" | custom-call | tf_op jit(solution)/shard_map/halo/pallas_call | solution.py:100
  14.9 16.5 %fit.1 = (f32[4,128,256]{2,1,0:T(8,128)}, f32[4,128,2048]{2,1,0:T(8,128)}, f32[4,128,128]{2,1,0:T(8,128)}, f32[2,128,128]{2,1,0:T(8,128)}) custom-call(s32[2]{0:T(128)} %pad_add_fusion.ids, s32[16,8]{1,0:T(8,128)} %copy.10.near, s32[16]{0:T(128)} %count.1, f32[48,4,256]{2,1,0:T(4,128)} %halo.1.window, s32[16,128]{1,0:T(8,128)} %skeleton.2, ...), custom_call_target="tpu_custom_call" | custom-call | tf_op jit(solution)/shard_map/fit/pallas_call | solution.py:228
  31.5 32.6 %exchange.1 = (f32[10,4,128,256]{3,2,1,0:T(8,128)}, s32[8,8,16,128]{3,2,1,0:T(8,128)}) custom-call(s32[8,128]{1,0:T(8,128)} %skeleton.3, s32[8]{0:T(128)} %owners.1, s32[8]{0:T(128)} %counts.1, f32[4,128,256]{2,1,0:T(8,128)} %get-tuple-element.10.fits), custom_call_target="tpu_custom_call" | custom-call | tf_op jit(solution)/shard_map/exchange/pallas_call | solution.py:413
  64.0 10.0 %level.1 = (f32[4,128,128]{2,1,0:T(8,128)}, f32[2,128,128]{2,1,0:T(8,128)}) custom-call(s32[2]{0:T(128)} %pad_add_fusion.ids, s32[16,8]{1,0:T(8,128)} %copy.10.near, f32[40,128,256]{2,1,0:T(8,128)} %bitcast.4, f32[4,128,2048]{2,1,0:T(8,128)} %get-tuple-element.13.left, f32[4,128,128]{2,1,0:T(8,128)} %get-tuple-element.14.block, ...), custom_call_target="tpu_custom_call" | custom-call | tf_op jit(solution)/shard_map/level/pallas_call | solution.py:479
  74.1 35.7 %route.1 = (f32[16,32,128]{2,1,0:T(8,128)}, f32[8,32,128]{2,1,0:T(8,128)}) custom-call(s32[64,16,128]{2,1,0:T(8,128)} %bitcast.6, f32[4,128,128]{2,1,0:T(8,128)} %get-tuple-element.16.one, f32[2,128,128]{2,1,0:T(8,128)} %get-tuple-element.17.two), custom_call_target="tpu_custom_call" | custom-call | tf_op jit(solution)/shard_map/route/pallas_call | solution.py:632
  109.8 1.7 %copy.14 = f32[16,32,128]{2,1,0:T(8,128)} copy(f32[16,32,128]{2,1,0:T(8,128)} %get-tuple-element.20) | data formatting | bytes 524288
  111.5 1.6 %copy.15 = f32[8,32,128]{2,1,0:T(8,128)} copy(f32[8,32,128]{2,1,0:T(8,128)} %get-tuple-element.21) | data formatting | bytes 262144

commit v3 on v0

v3 whole, which is shorter than its diff:
```python
import jax
import jax.numpy as jnp
from jax import lax
from jax.experimental import pallas as pl
from jax.experimental.pallas import tpu as pltpu
from jax.sharding import PartitionSpec as P

STEPS = 3
MESH = pl.DeviceIdType.MESH
F32 = jnp.float32
BF16 = jnp.bfloat16
NN = (((1,), (0,)), ((), ()))
NT = (((1,), (1,)), ((), ()))
TN = (((0,), (0,)), ((), ()))
MIB = 1 << 20

HOMES, MEMBERS = 64, 4
BOXES, MINE = 16, 4
PANELS, SLOTS, NEAR = 256, 128, 8
Z, W = 8, 8
ROWS = SLOTS // MEMBERS
PARTS = 2


def halves(x):
    high = x.astype(BF16)
    return high, (x - high.astype(F32)).astype(BF16)


def dot(a, b, dims):
    return lax.dot_general(a, b, dims, preferred_element_type=F32)


def dot3(a, b, dims):
    return dot(a[0], b[0], dims) + (dot(a[0], b[1], dims) + dot(a[1], b[0], dims))


def square(a, dims):
    cross = dot(a[0], a[1], dims)
    return dot(a[0], a[0], dims) + (cross + cross.T)


def within(index, count):
    return jnp.minimum(jnp.maximum(index, 0), count - 1)


def place():
    home, member = lax.axis_index("box"), lax.axis_index("blk")
    return home, member


def enter(peers):
    barrier = pltpu.get_barrier_semaphore()
    for peer in peers:
        pl.semaphore_signal(barrier, inc=1, device_id=peer, device_id_type=MESH)
    pl.semaphore_wait(barrier, len(peers))


def send(source, target, send_sem, recv_sem, peer):
    return pltpu.make_async_remote_copy(
        src_ref=source,
        dst_ref=target,
        send_sem=send_sem,
        recv_sem=recv_sem,
        device_id=peer,
        device_id_type=MESH,
    )


def home_at(across, along):
    return (across // 2) * 16 + along * 2 + lax.rem(across, 2)


def lines_of(home, member):
    across = 2 * (home // 16) + lax.rem(home, 2)
    along = lax.rem(home // 2, Z)
    line = [(home_at(across, lax.rem(along + d, Z)), member) for d in range(1, Z)]
    spots = [lax.rem(across + d, W) for d in range(1, W)]
    plane = [(spot, (home_at(spot, along), member)) for spot in spots]
    return line, plane, across, along


def refine(gram, right, chosen):
    steps = [1.0 / jnp.max(jnp.sum(jnp.abs(g), axis=1, keepdims=True), axis=0, keepdims=True) for g in gram]
    grams = [halves(g) for g in gram]
    fits = list(chosen)
    for _ in range(STEPS):
        updates = [r - dot3(g, halves(f), NN) for g, r, f in zip(grams, right, fits)]
        fits = [f + s * u for f, s, u in zip(fits, steps, updates)]
    return fits


def chosen_columns(row, count):
    position = lax.broadcasted_iota(jnp.int32, (2 * SLOTS, SLOTS), 0)
    slot = lax.broadcasted_iota(jnp.int32, (2 * SLOTS, SLOTS), 1)
    return jnp.where((position == row) & (slot < count), 1.0, 0.0).astype(F32)


def normal(square_matrix, columns):
    picks = columns.T
    picks16 = picks.astype(BF16)
    columns16 = columns.astype(BF16)
    high, low = halves(square_matrix)
    right = dot(picks16, high, NN) + dot(picks16, low, NN)
    high, low = halves(right)
    gram = dot(high, columns16, NN) + dot(low, columns16, NN)
    return gram, right, picks


def couple(col, row):
    total = None
    for axis in range(3):
        offset = col[axis] - row[axis]
        total = offset * offset if total is None else total + offset * offset
    return 0.03125 * lax.rsqrt(total + 0.01)


SCRATCH = [
    ("window", (3 * BOXES, 4, PANELS), F32),
    ("column", (3, PANELS, SLOTS), F32),
    ("high", (MINE, PANELS, NEAR * PANELS), BF16),
    ("low", (MINE, PANELS, NEAR * PANELS), BF16),
    ("fit_high", (MINE, SLOTS, PANELS), BF16),
    ("fit_low", (MINE, SLOTS, PANELS), BF16),
    ("left_high", (MINE, SLOTS, NEAR * PANELS), BF16),
    ("left_low", (MINE, SLOTS, NEAR * PANELS), BF16),
    ("reach", (10 * MINE, SLOTS, PANELS), F32),
    ("via", (MINE, SLOTS, PANELS), F32),
    ("blocks", (MINE, PANELS, PANELS), F32),
    ("block", (MINE, SLOTS, SLOTS), F32),
    ("pair", (MINE // 2, SLOTS, SLOTS), F32),
    ("cross_high", (SLOTS, NEAR * SLOTS), BF16),
    ("cross_low", (SLOTS, NEAR * SLOTS), BF16),
    ("one", (MINE, SLOTS, SLOTS), F32),
    ("merged", (MINE // 2, PANELS, PANELS), F32),
    ("two", (MINE // 2, SLOTS, SLOTS), F32),
    ("mine", (16, SLOTS), jnp.int32),
    ("table", (W, Z, 16, SLOTS), jnp.int32),
    ("lines0", (Z, 8, ROWS // PARTS, SLOTS), F32),
    ("lines1", (Z, 8, ROWS // PARTS, SLOTS), F32),
    ("packed", (PARTS, W - 1, 8, ROWS // PARTS, SLOTS), F32),
    ("arrived0", (W, 8, ROWS // PARTS, SLOTS), F32),
    ("arrived1", (W, 8, ROWS // PARTS, SLOTS), F32),
]
COPIES = [
    ("own", (8,)),
    ("halo_send", (2,)), ("halo_recv", (2,)),
    ("send", (5, MINE)), ("recv", (5, MINE)), ("give", (5, MINE)), ("take", (5, MINE)),
    ("table_line_send", (Z - 1,)), ("table_line_recv", (Z - 1,)),
    ("table_plane_send", (W - 1,)), ("table_plane_recv", (W - 1,)),
    ("row_send", (3,)), ("row_recv", (3,)), ("block_send", (PARTS, 3)), ("block_recv", (PARTS, 3)),
    ("up_send", (PARTS, 4)), ("up_recv", (PARTS, 4)), ("down_send", (PARTS, 4)), ("down_recv", (PARTS, 4)),
    ("plane_send", (PARTS, W - 1)), ("plane_recv", (PARTS, W - 1)),
]


class Refs:
    def __init__(self, refs):
        names = ["near", "owners"] + [name for name, *_ in SCRATCH] + [name + "_sem" for name, _ in COPIES]
        for name, ref in zip(names, refs, strict=True):
            setattr(self, name, ref)


def kernel(
    panels, self_blocks, neighbors, skeleton_one, count_one, skeleton_two, count_two, parent_at_slot, one_out, two_out, *refs
):
    v = Refs(refs)
    home, member = place()
    first = member * MINE
    boxes = range(MINE)
    side_hi, core = member // 2, lax.rem(member, 2)
    side_lo = lax.rem(home, 2)
    sign = 1 - 2 * side_hi
    outer = side_lo == side_hi
    flipped = home + 1 - 2 * side_lo
    side = (flipped, member)
    cross = (flipped, 2 * (1 - side_hi) + core)
    above = (lax.rem(home + 2 * sign + HOMES, HOMES), member)
    below = (lax.rem(home - 2 * sign + HOMES, HOMES), member)
    after = (lax.rem(home + 1, HOMES), member)
    before = (lax.rem(home + HOMES - 1, HOMES), member)
    sibling = (home, 2 * side_hi + 1 - core)
    members = [(home, lax.rem(member + d, MEMBERS)) for d in range(1, MEMBERS)]
    line, plane, across, along = lines_of(home, member)

    stage_near = pltpu.make_async_copy(neighbors, v.near, v.own_sem.at[0])
    stage_blocks = pltpu.make_async_copy(self_blocks.at[pl.ds(first, MINE)], v.blocks, v.own_sem.at[1])
    stage_panels = pltpu.make_async_copy(panels, v.window.at[pl.ds(BOXES, BOXES)], v.own_sem.at[2])
    stage_near.start()
    stage_panels.start()
    stage_blocks.start()

    lane = lax.broadcasted_iota(jnp.int32, (1, SLOTS), 1)
    owner_row = jnp.zeros((1, SLOTS), jnp.int32)
    count_row = jnp.zeros((1, SLOTS), jnp.int32)
    for s in range(8):
        owner_row = jnp.where(lane == s, parent_at_slot[s], owner_row)
        count_row = jnp.where(lane == s, count_two[s], count_row)
    v.mine[0:8, :] = skeleton_two[...]
    v.mine[8:16, :] = jnp.zeros((8, SLOTS), jnp.int32)
    v.mine[8:9, :] = owner_row
    v.mine[9:10, :] = count_row

    enter([after, before, cross, above, below] + members + line + [peer for _, peer in plane])

    halos = [
        send(panels, v.window.at[pl.ds(0, BOXES)], v.halo_send_sem.at[0], v.halo_recv_sem.at[0], after),
        send(panels, v.window.at[pl.ds(2 * BOXES, BOXES)], v.halo_send_sem.at[1], v.halo_recv_sem.at[1], before),
    ]
    for copy in halos:
        copy.start()

    spot = v.table.at[across, along]
    stage_table = pltpu.make_async_copy(v.mine, spot, v.own_sem.at[3])
    stage_table.start()
    table_line = [
        send(v.mine, spot, v.table_line_send_sem.at[i], v.table_line_recv_sem.at[i], peer) for i, peer in enumerate(line)
    ]
    for copy in table_line:
        copy.start()
    table_plane = [
        send(v.table.at[across], v.table.at[across], v.table_plane_send_sem.at[i], v.table_plane_recv_sem.at[i], peer)
        for i, (_, peer) in enumerate(plane)
    ]

    def slot(shift, k, to=1):
        return v.reach.at[MINE * (2 * (2 + to * sign * shift) + core) + k]

    def moved(source, target, stream, k, peer, recv):
        return send(source, target, v.send_sem.at[stream, k], v.recv_sem.at[recv, k], peer)

    def passed(shift, i, k):
        return send(slot(shift, k), slot(shift, k), v.give_sem.at[i, k], v.take_sem.at[i, k], sibling)

    def arrival(stream, k):
        return moved(slot(0, k), slot(0, k), stream, k, side, stream)

    def at_outer(body):
        pl.when(outer)(body)

    def at_inner(body):
        pl.when(jnp.logical_not(outer))(body)

    def outer_moves(k):
        return {
            "own": [
                moved(slot(0, k), slot(-2, k), 0, k, side, 0),
                moved(slot(0, k), v.via.at[k], 1, k, below, 1),
            ],
            "side": [moved(slot(2, k), slot(-2, k), 2, k, above, 2)]
            + ([moved(slot(2, k), slot(1, k, -1), 4, k, cross, 4)] if k % 2 else []),
            "next": [moved(v.via.at[k], slot(-1, k, -1), 3, k, cross, 3)],
        }

    def inner_moves(k):
        return {
            "own": [
                moved(slot(0, k), slot(2, k), 0, k, side, 0),
                moved(slot(0, k), slot(-1, k, -1), 1, k, cross, 1),
            ],
            "side": [
                moved(slot(-2, k), slot(1, k, -1), 2, k, cross, 2),
                moved(slot(-2, k), slot(2, k), 3, k, below, 3),
            ],
            "next": [moved(slot(-1, k), slot(1, k), 4, k, side, 4)] if k % 2 == 0 else [],
        }

    def begin(copies):
        for copy in copies:
            copy.start()

    def send_own(k):
        at_outer(lambda: begin(outer_moves(k)["own"]))
        at_inner(lambda: begin(inner_moves(k)["own"]))
        passed(0, 4, k).start()

    def early(k):
        @at_outer
        def _():
            arrival(0, k).wait_recv()
            begin(outer_moves(k)["side"] + [passed(2, 0, k)])
            arrival(1, k).wait_recv()
            begin(outer_moves(k)["next"])

        @at_inner
        def _():
            arrival(0, k).wait_recv()
            begin(inner_moves(k)["side"] + [passed(-2, 0, k)])
            arrival(1, k).wait_recv()
            begin(inner_moves(k)["next"] + [passed(-1, 1, k)])

    def late(k):
        @at_outer
        def _():
            for stream, shift, i in ((2, -2, 1), (3, -1, 2), (4, 1, 3)):
                arrival(stream, k).wait_recv()
                passed(shift, i, k).start()

        @at_inner
        def _():
            for stream, shift, i in ((2, 1, 2), (3, 2, 3)):
                arrival(stream, k).wait_recv()
                passed(shift, i, k).start()

    def taken():
        for k in boxes:
            for i in range(5):
                passed(0, i, k).wait_recv()

    def sent():
        for k in boxes:

            @at_outer
            def _():
                for copies in outer_moves(k).values():
                    for copy in copies:
                        copy.wait_send()

            @at_inner
            def _():
                for copies in inner_moves(k).values():
                    for copy in copies:
                        copy.wait_send()

            for i in range(5):
                passed(0, i, k).wait_send()

    tile = 64

    def couple_with(box, write):
        for part in range(PANELS // SLOTS):
            lanes = slice(part * SLOTS, (part + 1) * SLOTS)
            row = [v.window[box, axis : axis + 1, lanes] for axis in range(3)]
            for start in range(0, PANELS, tile):
                col = [v.column[axis, start : start + tile, :] for axis in range(3)]
                hi, lo = halves(couple(col, row))
                write(start, part, hi, lo)

    def columns_of(own):
        for axis in range(3):
            row = v.window[BOXES + first + own, axis : axis + 1, :]
            v.column[axis] = jnp.broadcast_to(row, (SLOTS, PANELS)).T

    def split_fit(own):
        return v.fit_high[own], v.fit_low[own]

    def fit_box(own):
        columns_of(own)

        def proxy(index, carry):
            box = within(v.near[first + own, index] - (home - 1) * BOXES, 3 * BOXES)

            def write(start, part, hi, lo):
                lanes = pl.ds(pl.multiple_of(index * PANELS + part * SLOTS, SLOTS), SLOTS)
                v.high[own, start : start + tile, lanes] = hi
                v.low[own, start : start + tile, lanes] = lo

            couple_with(box, write)
            return carry

        lax.fori_loop(0, NEAR, proxy, 0)
        columns = chosen_columns(skeleton_one[pl.ds(first + own, 1), :], count_one[first + own])
        gram, right, pick = normal(square((v.high[own], v.low[own]), NT), columns)
        (fit,) = refine([gram], [right], [pick])
        weight = jnp.sum(fit * fit * v.window[BOXES + first + own, 3:4, :], axis=1, keepdims=True)
        v.reach[MINE * (4 + core) + own] = fit * lax.rsqrt(jnp.maximum(weight, 1.0))
        v.fit_high[own], v.fit_low[own] = halves(fit)

    def left_box(own):
        for index in range(NEAR):
            lanes = slice(index * PANELS, (index + 1) * PANELS)
            product = dot3(split_fit(own), (v.high[own, :, lanes], v.low[own, :, lanes]), NN)
            v.left_high[own, :, lanes], v.left_low[own, :, lanes] = halves(product)
        part = dot3(split_fit(own), halves(v.blocks[own]), NN)
        v.block[own] = dot3(halves(part), split_fit(own), NT)

    def pair_of(j):
        a, e = 2 * j, 2 * j + 1
        columns_of(a)

        def write(start, part, hi, lo):
            lanes = slice(part * SLOTS, (part + 1) * SLOTS)
            v.high[a, start : start + tile, lanes] = hi
            v.low[a, start : start + tile, lanes] = lo

        couple_with(BOXES + first + e, write)
        part = dot3(split_fit(a), (v.high[a, :, :PANELS], v.low[a, :, :PANELS]), NN)
        v.pair[j] = dot3(halves(part), split_fit(e), NT)

    stage_near.wait()
    stage_panels.wait()
    for copy in halos:
        copy.wait_recv()
    fit_box(0)
    send_own(0)
    fit_box(1)
    send_own(1)
    early(0)
    for copy in table_line:
        copy.wait_recv()
    stage_table.wait()
    begin(table_plane)
    fit_box(2)
    send_own(2)
    early(1)
    late(0)
    fit_box(3)
    send_own(3)
    early(2)
    late(1)
    stage_blocks.wait()
    left_box(0)
    left_box(1)
    early(3)
    late(2)
    pair_of(0)
    left_box(2)
    left_box(3)
    pair_of(1)
    late(3)
    for copy in table_plane:
        copy.wait_recv()
    listing = pltpu.make_async_copy(v.table.at[:, :, 8], v.owners, v.own_sem.at[4])
    listing.start()
    taken()

    base = 16 * home + 8 * side_hi - 16
    for own in boxes:
        for index in range(NEAR):
            box = within(v.near[first + own, index] - base, 10 * MINE)
            lanes = slice(index * PANELS, (index + 1) * PANELS)
            left = (v.left_high[own, :, lanes], v.left_low[own, :, lanes])
            lanes = slice(index * SLOTS, (index + 1) * SLOTS)
            v.cross_high[:, lanes], v.cross_low[:, lanes] = halves(dot3(left, halves(v.reach[box]), NT))
        v.one[own] = v.block[own] - square((v.cross_high[...], v.cross_low[...]), NT)

    def rows(array, target, first_row, count):
        return array.at[:, pl.ds(pl.multiple_of(target * ROWS + first_row, count), count), :]

    mine_one = one_out.at[pl.ds(MINE * member, MINE)]
    own_one = pltpu.make_async_copy(rows(v.one, member, 0, ROWS), mine_one, v.own_sem.at[5])
    ones = [
        send(rows(v.one, peer[1], 0, ROWS), mine_one, v.row_send_sem.at[i], v.row_recv_sem.at[i], peer)
        for i, peer in enumerate(members)
    ]
    begin(ones + [own_one])

    grams, rights, picks, bodies = [], [], [], []
    for j in range(MINE // 2):
        between = v.pair[j]
        v.merged[j, :SLOTS, :SLOTS] = v.one[2 * j]
        v.merged[j, :SLOTS, SLOTS:] = between
        v.merged[j, SLOTS:, :SLOTS] = between.T
        v.merged[j, SLOTS:, SLOTS:] = v.one[2 * j + 1]
        body = halves(v.merged[j])
        parent = (home * BOXES + first) // 2 + j
        lane = lax.broadcasted_iota(jnp.int32, (W * Z, SLOTS), 1)
        table = v.table.reshape(W * Z, 16, SLOTS)
        found = ((table[:, 8, :] == parent) & (lane < 8)).astype(F32)
        row = jnp.zeros((1, SLOTS), F32)
        for s in range(8):
            row = row + jnp.sum(found[:, s : s + 1] * table[:, s, :].astype(F32), axis=0, keepdims=True)
        count = jnp.sum(jnp.sum(found * table[:, 9, :].astype(F32), axis=0, keepdims=True), axis=1, keepdims=True)
        columns = chosen_columns(row.astype(jnp.int32), count.astype(jnp.int32))
        gram, right, pick = normal(square(body, TN), columns)
        grams.append(gram)
        rights.append(right)
        picks.append(pick)
        bodies.append(body)
    fits = refine(grams, rights, picks)
    for j in range(MINE // 2):
        fit = halves(fits[j])
        v.two[j] = dot3(halves(dot3(fit, bodies[j], NN)), fit, NT)

    up, down = line[0], line[-1]
    half = ROWS // PARTS
    lines, arrived = (v.lines0, v.lines1), (v.arrived0, v.arrived1)

    def ours(part):
        return lines[part].at[along, pl.ds(2 * member, 2)]

    own_two = [
        pltpu.make_async_copy(rows(v.two, member, part * half, half), ours(part), v.own_sem.at[6 + part])
        for part in range(PARTS)
    ]
    parts = [
        [
            send(
                rows(v.two, peer[1], part * half, half),
                ours(part),
                v.block_send_sem.at[part, i],
                v.block_recv_sem.at[part, i],
                peer,
            )
            for i, peer in enumerate(members)
        ]
        for part in range(PARTS)
    ]
    for part in range(PARTS):
        begin(parts[part] + [own_two[part]])

    def upward(part, step):
        spot = lines[part].at[lax.rem(along - step + Z, Z)]
        return send(spot, spot, v.up_send_sem.at[part, step], v.up_recv_sem.at[part, step], up)

    def downward(part, step):
        spot = lines[part].at[lax.rem(along + step, Z)]
        return send(spot, spot, v.down_send_sem.at[part, step], v.down_recv_sem.at[part, step], down)

    def steps(part):
        return (4, 3) if part % 2 == 0 else (3, 4)

    def gather(part, step):
        for way, copy in enumerate((upward, downward)):
            if step and step - 1 < steps(part)[way]:
                copy(part, step - 1).wait_recv()
            if step < steps(part)[way]:
                copy(part, step).start()

    def pack(target, at):
        for s in range(8):
            parent = v.owners[at, along, s]
            source = parent // 8
            target(s, lax.rem(source // 2, Z), lax.rem(parent, 8))

    def across_copy(part, i):
        return send(
            v.packed.at[part, i],
            arrived[part].at[across],
            v.plane_send_sem.at[part, i],
            v.plane_recv_sem.at[part, i],
            plane[i][1],
        )

    def send_across(part):
        for i, (spot, _) in enumerate(plane):

            def put(s, z, j):
                v.packed[part, i, s] = lines[part][z, j]

            pack(put, spot)
            across_copy(part, i).start()

        def put(s, z, j):
            arrived[part][across, s] = lines[part][z, j]

        pack(put, across)

    listing.wait()
    for part in range(PARTS):
        own_two[part].wait()
        for copy in parts[part]:
            copy.wait_recv()
        gather(part, 0)
    for step in range(1, 6):
        if step < 5:
            gather(0, step)
        if step > 1:
            gather(1, step - 1)
        if step > 3:
            send_across(step - 4)
    for part in range(PARTS):
        for i in range(W - 1):
            across_copy(part, i).wait_recv()
        for s in range(8):
            source = v.owners[across, along, s] // 8
            two_out[s, part * half : (part + 1) * half, :] = arrived[part][2 * (source // 16) + lax.rem(source, 2), s]

    own_one.wait()
    for copy in ones:
        copy.wait()
    sent()
    for copy in halos + table_line + table_plane:
        copy.wait_send()
    for part in range(PARTS):
        for copy in parts[part]:
            copy.wait_send()
        for step in range(4):
            for way, copy in enumerate((upward, downward)):
                if step < steps(part)[way]:
                    copy(part, step).wait_send()
        for i in range(W - 1):
            across_copy(part, i).wait_send()


def local(panels, self_blocks, neighbors, skeleton_one, count_one, skeleton_two, count_two, parent_at_slot):
    hbm = pl.BlockSpec(memory_space=pl.ANY)
    vmem = pl.BlockSpec(memory_space=pltpu.VMEM)
    smem = pl.BlockSpec(memory_space=pltpu.SMEM)
    return pl.pallas_call(
        kernel,
        out_shape=[
            jax.ShapeDtypeStruct((BOXES, ROWS, SLOTS), F32),
            jax.ShapeDtypeStruct((8, ROWS, SLOTS), F32),
        ],
        in_specs=[hbm, hbm, hbm, vmem, smem, vmem, smem, smem],
        out_specs=[hbm, vmem],
        scratch_shapes=[
            pltpu.SMEM((BOXES, NEAR), jnp.int32),
            pltpu.SMEM((W, Z, SLOTS), jnp.int32),
            *(pltpu.VMEM(shape, dtype) for _, shape, dtype in SCRATCH),
            *(pltpu.SemaphoreType.DMA(shape) for _, shape in COPIES),
        ],
        compiler_params=pltpu.CompilerParams(collective_id=0, has_side_effects=True, vmem_limit_bytes=56 * MIB),
        name="skeletonize",
    )(panels, self_blocks, neighbors, skeleton_one, count_one, skeleton_two, count_two, parent_at_slot)


def solution(mesh):
    placed = (
        P("box", None, None),
        P("box", None, None),
        P("box", None),
        P("box", None),
        P("box"),
        P("box", None),
        P("box"),
        P("box"),
    )
    return jax.shard_map(
        local,
        mesh=mesh,
        in_specs=placed,
        out_specs=(P("box", "blk", None), P("box", "blk", None)),
        check_vma=False,
    )
```

time: 1480 us -> 92.1 us (0.06)
  waiting for transfers between devices: 1030 us -> 0 us
  local copies, waits for them, and re-layouts: 169 us -> 4.59 us
  matrix products: 143 us -> 0 us
  Pallas kernels: 0 us -> 85.1 us
  loops' own time: 72.1 us -> 0 us
  other arithmetic: 39 us -> 0 us
    all_gather x1 -> x0, waiting for transfers between devices: 725 us -> none  [local(): lax.all_gather(part, 'box', axis=0, tiled=True)]
    dot_general x171 -> x0, matrix products: 143 us -> none  [the longest x17 26.8 us: normal_terms(): right_part = jnp.dot(picked_cols.T, proxy_kernel, precision=precise)]
    psum x2 -> x0, waiting for transfers between devices: 139 us -> none  [the longest x1 83.3 us: local(): gram_part, right_part = lax.psum((gram_part, right_part), 'blk')]
    gather x83 -> x0, local copies, waits for them, and re-layouts: 102 us -> none  [the longest x16 53.6 us: coarse(): near_fits = far_fits[near_cols]]
    ppermute x4 -> x0, waiting for transfers between devices: 91.9 us -> none  [the longest x2 87.4 us: with_halo(): lax.ppermute(tail, axis, [(i, (i + 1) % count) for i in range(ends)])]
    pallas_call x0 -> x1, Pallas kernels: none -> 85.1 us  [local(): pl.pallas_call(kernel, out_shape=[jax.ShapeDtypeStruct((BOXES, ROWS, SLOT...]
    another operation x3 -> x0, loops' own time: 72.1 us -> none  [the longest x1 34.9 us: local(): block_rows, schur_term = lax.map(coarse, jnp.arange(box_count))]
    reduce_scatter x2 -> x0, waiting for transfers between devices: 69.3 us -> none  [the longest x1 36 us: local(): lax.psum_scatter(schur_term, 'blk', scatter_dimension=1, tiled=True)]
  transfers between devices with their start and end apart: 9 -> 0, of which waited for: 8 -> 0; matrix products, arithmetic and copies ran while one was open for 0% -> 0% of each run, Pallas kernels for 0% -> 0%
where the time goes in v3:
time: 92.1 us; the launch traced here: 90.3 us
  Pallas kernels  85.1 us (92%)
  local copies, waits for them, and re-layouts  4.59 us (5%)
    pallas_call x1, Pallas kernels, local(): pl.pallas_call(kernel, out_shape=[jax.ShapeDtypeStruct((BOXES, ROWS, SLOT...  85.1 us
    unnamed x3, local copies, waits for them, and re-layouts  4.59 us

profile of v3, /device:TPU:2, one launch (start us, length us, event | category | flops | bytes accessed | tf_op | source)
XLA Modules:
  0.0 90.3 jit_solution(10622944354110472440)
XLA Ops:
  0.6 1.4 %copy.10.neighbors = s32[16,8]{1,0:T(8,128)} copy(s32[16,8]{0,1:T(8,128)} %param.10) | data formatting | bytes 1024 | tf_op args[2]
  2.0 85.1 %skeletonize.1 = (f32[16,32,128]{2,1,0:T(8,128)}, f32[8,32,128]{2,1,0:T(8,128)}) custom-call(f32[16,4,256]{2,1,0:T(4,128)} %panels.1, f32[16,256,256]{2,1,0:T(8,128)} %self_blocks.1, s32[16,8]{1,0:T(8,128)} %copy.10.neighbors, s32[16,128]{1,0:T(8,128)} %skeleton_one.1, s32[16]{0:T(128)} %count_one.1, s32[8,128]{1,0:T(8,128)} %skeleton_two.1, s32[8]{0:T(128)} %count_two.1, ...), custom_call_target="tpu_custom_call" | custom-call | tf_op jit(solution)/shard_map/skeletonize/pallas_call | solution.py:590
  87.1 1.7 %copy.13 = f32[16,32,128]{2,1,0:T(8,128)} copy(f32[16,32,128]{2,1,0:T(8,128)} %get-tuple-element.4) | data formatting | bytes 524288
  88.7 1.6 %copy.14 = f32[8,32,128]{2,1,0:T(8,128)} copy(f32[8,32,128]{2,1,0:T(8,128)} %get-tuple-element.5) | data formatting | bytes 262144

commit v4 on v3

v4 whole, which is shorter than its diff:
```python
import jax
import jax.numpy as jnp
from jax import lax
from jax.experimental import pallas as pl
from jax.experimental.pallas import tpu as pltpu
from jax.sharding import PartitionSpec as P

STEPS = 3
MESH = pl.DeviceIdType.MESH
F32 = jnp.float32
BF16 = jnp.bfloat16
NN = (((1,), (0,)), ((), ()))
NT = (((1,), (1,)), ((), ()))
TN = (((0,), (0,)), ((), ()))
MIB = 1 << 20

HOMES, MEMBERS = 64, 4
BOXES, MINE = 16, 4
PANELS, SLOTS, NEAR = 256, 128, 8
Z, W = 8, 8
ROWS = SLOTS // MEMBERS
ROUND, OTHER = 0, 1


def halves(x):
    high = x.astype(BF16)
    return high, (x - high.astype(F32)).astype(BF16)


def dot(a, b, dims):
    return lax.dot_general(a, b, dims, preferred_element_type=F32)


def dot3(a, b, dims):
    return dot(a[0], b[0], dims) + (dot(a[0], b[1], dims) + dot(a[1], b[0], dims))


def square(a, dims):
    cross = dot(a[0], a[1], dims)
    return dot(a[0], a[0], dims) + (cross + cross.T)


def within(index, count):
    return jnp.minimum(jnp.maximum(index, 0), count - 1)


def place():
    home, member = lax.axis_index("box"), lax.axis_index("blk")
    return home, member


def enter(peers):
    barrier = pltpu.get_barrier_semaphore()
    for peer in peers:
        pl.semaphore_signal(barrier, inc=1, device_id=peer, device_id_type=MESH)
    pl.semaphore_wait(barrier, len(peers))


def send(source, target, send_sem, recv_sem, peer):
    return pltpu.make_async_remote_copy(
        src_ref=source,
        dst_ref=target,
        send_sem=send_sem,
        recv_sem=recv_sem,
        device_id=peer,
        device_id_type=MESH,
    )


def home_at(across, along):
    return (across // 2) * 16 + along * 2 + lax.rem(across, 2)


def lines_of(home, member):
    across = 2 * (home // 16) + lax.rem(home, 2)
    along = lax.rem(home // 2, Z)
    line = [(home_at(across, lax.rem(along + d, Z)), member) for d in range(1, Z)]
    spots = [lax.rem(across + d, W) for d in range(1, W)]
    plane = [(spot, (home_at(spot, along), member)) for spot in spots]
    return line, plane, across, along


def refine(gram, right, chosen):
    steps = [1.0 / jnp.max(jnp.sum(jnp.abs(g), axis=1, keepdims=True), axis=0, keepdims=True) for g in gram]
    grams = [halves(g) for g in gram]
    fits = list(chosen)
    for _ in range(STEPS):
        updates = [r - dot3(g, halves(f), NN) for g, r, f in zip(grams, right, fits)]
        fits = [f + s * u for f, s, u in zip(fits, steps, updates)]
    return fits


def chosen_columns(row, count):
    position = lax.broadcasted_iota(jnp.int32, (2 * SLOTS, SLOTS), 0)
    slot = lax.broadcasted_iota(jnp.int32, (2 * SLOTS, SLOTS), 1)
    return jnp.where((position == row) & (slot < count), 1.0, 0.0).astype(F32)


def normal(square_matrix, columns):
    picks = columns.T
    picks16 = picks.astype(BF16)
    columns16 = columns.astype(BF16)
    high, low = halves(square_matrix)
    right = dot(picks16, high, NN) + dot(picks16, low, NN)
    high, low = halves(right)
    gram = dot(high, columns16, NN) + dot(low, columns16, NN)
    return gram, right, picks


def couple(col, row):
    total = None
    for axis in range(3):
        offset = col[axis] - row[axis]
        total = offset * offset + (1024.0 * 0.01 if total is None else total)
    return lax.rsqrt(total)


SCRATCH = [
    ("window", (3 * BOXES, 4, PANELS), F32),
    ("column", (2, 3, PANELS, SLOTS), F32),
    ("couples", (MINE + 2, 2 * PANELS, NEAR * PANELS), BF16),
    ("siblings", (MINE // 2, 2 * PANELS, PANELS), BF16),
    ("fit_high", (MINE, SLOTS, PANELS), BF16),
    ("fit_low", (MINE, SLOTS, PANELS), BF16),
    ("left_high", (MINE, SLOTS, NEAR * PANELS), BF16),
    ("left_low", (MINE, SLOTS, NEAR * PANELS), BF16),
    ("reach", (10 * MINE, SLOTS, PANELS), F32),
    ("via", (MINE, SLOTS, PANELS), F32),
    ("round", (SLOTS, PANELS), F32),
    ("blocks", (MINE, PANELS, PANELS), F32),
    ("block", (MINE, SLOTS, SLOTS), F32),
    ("pair", (MINE // 2, SLOTS, SLOTS), F32),
    ("cross_high", (MINE, SLOTS, NEAR * SLOTS), BF16),
    ("cross_low", (MINE, SLOTS, NEAR * SLOTS), BF16),
    ("one", (MINE, SLOTS, SLOTS), F32),
    ("merged", (MINE // 2, PANELS, PANELS), F32),
    ("two", (MINE // 2, SLOTS, SLOTS), F32),
    ("mine", (16, SLOTS), F32),
    ("line_tables", (Z, 16, SLOTS), F32),
    ("ours", (8, SLOTS), jnp.int32),
    ("plane_tables", (W, 8, SLOTS), jnp.int32),
    ("answers", (W, 16, SLOTS), F32),
    ("heard", (W, 16, SLOTS), F32),
    ("lines00", (Z, MEMBERS, ROWS // 2, SLOTS), F32),
    ("lines01", (Z, MEMBERS, ROWS // 2, SLOTS), F32),
    ("lines10", (Z, MEMBERS, ROWS // 2, SLOTS), F32),
    ("lines11", (Z, MEMBERS, ROWS // 2, SLOTS), F32),
    ("packed", (2, W, 8, ROWS // 2, SLOTS), F32),
]
COPIES = [
    ("own", (9,)),
    ("halo_send", (2,)), ("halo_recv", (2,)),
    ("send", (7, MINE)), ("recv", (6, MINE)), ("give", (5, MINE)), ("take", (5, MINE)),
    ("table_send", (2, 7)), ("table_recv", (2, 7)), ("answer_send", (7,)), ("answer_recv", (7,)),
    ("row_send", (3,)), ("row_recv", (3,)), ("block_send", (4, 3)), ("block_recv", (4, 3)),
    ("up_send", (4, 4)), ("up_recv", (4, 4)), ("down_send", (4, 4)), ("down_recv", (4, 4)),
    ("plane_send", (2, 7)), ("plane_recv", (2, 7)),
]


class Refs:
    def __init__(self, refs):
        names = ["near", "owners"] + [name for name, *_ in SCRATCH] + [name + "_sem" for name, _ in COPIES]
        for name, ref in zip(names, refs, strict=True):
            setattr(self, name, ref)


def kernel(
    panels, self_blocks, neighbors, skeleton_one, count_one, skeleton_two, count_two, parent_at_slot, one_out, arrived, *refs
):
    v = Refs(refs)
    home, member = place()
    first = member * MINE
    boxes = range(MINE)
    side_hi, core = member // 2, lax.rem(member, 2)
    side_lo = lax.rem(home, 2)
    sign = 1 - 2 * side_hi
    outer = side_lo == side_hi
    flipped = home + 1 - 2 * side_lo
    side = (flipped, member)
    cross = (flipped, 2 * (1 - side_hi) + core)
    above = (lax.rem(home + 2 * sign + HOMES, HOMES), member)
    below = (lax.rem(home - 2 * sign + HOMES, HOMES), member)
    after = (lax.rem(home + 1, HOMES), member)
    before = (lax.rem(home + HOMES - 1, HOMES), member)
    sibling = (home, 2 * side_hi + 1 - core)
    members = [(home, lax.rem(member + d, MEMBERS)) for d in range(1, MEMBERS)]
    line, plane, across, along = lines_of(home, member)

    stage_near = pltpu.make_async_copy(neighbors, v.near, v.own_sem.at[0])
    stage_blocks = pltpu.make_async_copy(self_blocks.at[pl.ds(first, MINE)], v.blocks, v.own_sem.at[1])
    stage_panels = pltpu.make_async_copy(panels, v.window.at[pl.ds(BOXES, BOXES)], v.own_sem.at[2])
    stage_near.start()
    stage_panels.start()
    stage_blocks.start()

    lane = lax.broadcasted_iota(jnp.int32, (1, SLOTS), 1)
    nothing = jnp.full((1, SLOTS), -1.0, F32)
    owner_row, count_row, plain_row = nothing, nothing, jnp.zeros((1, SLOTS), jnp.int32)
    for s in range(8):
        owner_row = jnp.where(lane == 8 * along + s, parent_at_slot[s].astype(F32), owner_row)
        plain_row = jnp.where(lane == s, parent_at_slot[s], plain_row)
        count_row = jnp.where(lane == 8 * along + s, count_two[s].astype(F32), count_row)
    v.mine[0:8, :] = skeleton_two[...].astype(F32)
    v.mine[8:9, :] = owner_row
    v.mine[9:10, :] = count_row
    v.mine[10:16, :] = jnp.zeros((6, SLOTS), F32)
    v.ours[...] = jnp.broadcast_to(plain_row, (8, SLOTS))

    enter([after, before, cross, above, below] + members + line + [peer for _, peer in plane])

    halos = [
        send(panels, v.window.at[pl.ds(0, BOXES)], v.halo_send_sem.at[0], v.halo_recv_sem.at[0], after),
        send(panels, v.window.at[pl.ds(2 * BOXES, BOXES)], v.halo_send_sem.at[1], v.halo_recv_sem.at[1], before),
    ]
    for copy in halos:
        copy.start()

    spots = [(v.mine, v.line_tables.at[along]), (v.ours, v.plane_tables.at[across])]
    stage_tables = [pltpu.make_async_copy(*spot, v.own_sem.at[3 + i]) for i, spot in enumerate(spots)]
    tables = [
        send(*spots[way], v.table_send_sem.at[way, i], v.table_recv_sem.at[way, i], peer)
        for way, peers in enumerate((line, [peer for _, peer in plane]))
        for i, peer in enumerate(peers)
    ]
    answers = [
        send(v.answers.at[at], v.heard.at[across], v.answer_send_sem.at[i], v.answer_recv_sem.at[i], peer)
        for i, (at, peer) in enumerate(plane)
    ]
    listing = pltpu.make_async_copy(v.plane_tables.at[:, 0], v.owners, v.own_sem.at[5])

    def answer():
        for copy in tables:
            copy.wait_recv()
        for copy in stage_tables:
            copy.wait()
        listing.start()
        owner_row = jnp.max(v.line_tables[:, 8, :], axis=0, keepdims=True)
        count_row = jnp.max(v.line_tables[:, 9, :], axis=0, keepdims=True)
        row = lax.broadcasted_iota(jnp.int32, (8 * W, SLOTS), 0)
        at = row >> 3
        parent = 8 * ((at >> 1) * 16 + along * 2 + (at & 1)) + (row & 7)
        found = jnp.where(owner_row == parent.astype(F32), 1.0, 0.0).astype(F32)
        skeletons = jnp.concatenate([v.line_tables[z, 0:8, :] for z in range(Z)], axis=0)
        skeletons = jnp.concatenate([skeletons, jnp.zeros_like(skeletons)], axis=0)
        chosen = dot(found.astype(BF16), skeletons.astype(BF16), NN)
        counts = jnp.broadcast_to(jnp.sum(found * count_row, axis=1, keepdims=True), chosen.shape)
        for at in range(W):
            v.answers[at, 0:8, :] = chosen[8 * at : 8 * at + 8, :]
            v.answers[at, 8:16, :] = counts[8 * at : 8 * at + 8, :]
        v.heard[across] = v.answers[across]
        begin(answers)

    def begin(copies):
        for copy in copies:
            copy.start()

    begin(tables + stage_tables)

    def slot(shift, k, to=1):
        return v.reach.at[MINE * (2 * (2 + to * sign * shift) + core) + k]

    def moved(source, target, stream, k, peer, recv):
        return send(source, target, v.send_sem.at[stream, k], v.recv_sem.at[recv, k], peer)

    def passed(shift, i, k):
        return send(slot(shift, k), slot(shift, k), v.give_sem.at[i, k], v.take_sem.at[i, k], sibling)

    def arrival(stream, k):
        return moved(slot(0, k), slot(0, k), stream, k, side, stream)

    def at_outer(body):
        pl.when(outer)(body)

    def at_inner(body):
        pl.when(jnp.logical_not(outer))(body)

    def outer_moves(k):
        return {
            "own": [
                moved(slot(0, k), slot(-2, k), 0, k, side, 0),
                moved(slot(0, k), v.via.at[k], 1, k, below, 1),
            ]
            + ([moved(slot(0, k), v.round, 5, k, cross, 5)] if k == ROUND else []),
            "side": [moved(slot(2, k), slot(-2, k), 2, k, above, 2)]
            + ([moved(slot(2, k), slot(1, k, -1), 4, k, cross, 4)] if k == OTHER else []),
            "next": [moved(v.via.at[k], slot(-1, k, -1), 3, k, cross, 3)]
            + ([moved(v.round, slot(1, k), 6, k, side, 2)] if k == ROUND else []),
        }

    def inner_moves(k):
        return {
            "own": [
                moved(slot(0, k), slot(2, k), 0, k, side, 0),
                moved(slot(0, k), slot(-1, k, -1), 1, k, cross, 1),
            ],
            "side": ([moved(slot(-2, k), slot(1, k, -1), 2, k, cross, 2)] if k != ROUND else [])
            + [moved(slot(-2, k), slot(2, k), 3, k, below, 3)],
            "next": [moved(slot(-1, k), slot(1, k), 4, k, side, 4)] if k != OTHER else [],
        }

    def send_own(k):
        at_outer(lambda: begin(outer_moves(k)["own"]))
        at_inner(lambda: begin(inner_moves(k)["own"]))
        passed(0, 4, k).start()

    def early(k):
        @at_outer
        def _():
            arrival(0, k).wait_recv()
            begin(outer_moves(k)["side"] + [passed(2, 0, k)])
            arrival(1, k).wait_recv()
            if k == ROUND:
                arrival(5, k).wait_recv()
            begin(outer_moves(k)["next"])

        @at_inner
        def _():
            arrival(0, k).wait_recv()
            begin(inner_moves(k)["side"] + [passed(-2, 0, k)])
            arrival(1, k).wait_recv()
            begin(inner_moves(k)["next"] + [passed(-1, 1, k)])

    def late(k):
        @at_outer
        def _():
            for stream, shift, i in ((2, -2, 1), (3, -1, 2), (4, 1, 3)):
                arrival(stream, k).wait_recv()
                passed(shift, i, k).start()

        @at_inner
        def _():
            for stream, shift, i in ((2, 1, 2), (3, 2, 3)):
                arrival(stream, k).wait_recv()
                passed(shift, i, k).start()

    def taken():
        for k in boxes:
            for i in range(5):
                passed(0, i, k).wait_recv()

    def sent():
        for k in boxes:

            @at_outer
            def _():
                for copies in outer_moves(k).values():
                    for copy in copies:
                        copy.wait_send()

            @at_inner
            def _():
                for copies in inner_moves(k).values():
                    for copy in copies:
                        copy.wait_send()

            for i in range(5):
                passed(0, i, k).wait_send()

    tile = 64

    def columns_of(box, turn):
        for axis in range(3):
            row = 32.0 * v.window[BOXES + box, axis : axis + 1, :]
            v.column[turn, axis] = jnp.broadcast_to(row, (SLOTS, PANELS)).T

    def couple_with(turn, box, target, first_lane):
        for part in range(PANELS // SLOTS):
            lanes = slice(part * SLOTS, (part + 1) * SLOTS)
            row = [32.0 * v.window[box, axis : axis + 1, lanes] for axis in range(3)]
            lanes = slice(first_lane + part * SLOTS, first_lane + (part + 1) * SLOTS)
            for start in range(0, PANELS, tile):
                col = [v.column[turn, axis, start : start + tile, :] for axis in range(3)]
                hi, lo = halves(couple(col, row))
                target[start : start + tile, lanes] = hi
                target[PANELS + start : PANELS + start + tile, lanes] = lo

    order = [(first + k, slot(0, k), k) for k in boxes]

    def proxies(i, indices):
        box, _, room = order[i]
        for index in indices:
            near = within(v.near[index, box] - (home - 1) * BOXES, 3 * BOXES)
            couple_with(i % 2, near, v.couples.at[room], index * PANELS)

    def products(room, half):
        lanes = slice(half * (NEAR * PANELS // 2), (half + 1) * (NEAR * PANELS // 2))
        return dot(v.couples[room, :, lanes], v.couples[room, :PANELS, lanes], NT)

    def fit_box(i):
        box, spot, room = order[i]
        more = i + 1 < len(order)
        if more:
            columns_of(order[i + 1][0], (i + 1) % 2)
        total = products(room, 0)
        if more:
            proxies(i + 1, (0, 1, 2))
        total = total + products(room, 1)
        if more:
            proxies(i + 1, (3, 4, 5))
        low = total[PANELS:]
        columns = chosen_columns(skeleton_one[pl.ds(box, 1), :], count_one[box])
        gram, right, pick = normal(total[:PANELS] + (low + low.T), columns)
        (fit,) = refine([gram], [right], [pick])
        if more:
            proxies(i + 1, (6, 7))
        weight = jnp.sum(fit * fit * v.window[BOXES + box, 3:4, :], axis=1, keepdims=True)
        spot[...] = fit * lax.rsqrt(jnp.maximum(weight, 1.0))
        if i < MINE:
            v.fit_high[i], v.fit_low[i] = halves(fit)

    def split_fit(own):
        return v.fit_high[own], v.fit_low[own]

    def left_box(own):
        for index in range(NEAR):
            lanes = slice(index * PANELS, (index + 1) * PANELS)
            product = dot3(split_fit(own), (v.couples[own, :PANELS, lanes], v.couples[own, PANELS:, lanes]), NN)
            v.left_high[own, :, lanes], v.left_low[own, :, lanes] = halves(product)
        part = dot3(split_fit(own), halves(v.blocks[own]), NN)
        v.block[own] = dot3(halves(part), split_fit(own), NT)

    def pair_of(j):
        a, e = 2 * j, 2 * j + 1
        columns_of(first + a, j)
        couple_with(j, BOXES + first + e, v.siblings.at[j], 0)
        part = dot3(split_fit(a), (v.siblings[j, :PANELS, :], v.siblings[j, PANELS:, :]), NN)
        v.pair[j] = dot3(halves(part), split_fit(e), NT)

    stage_near.wait()
    stage_panels.wait()
    for copy in halos:
        copy.wait_recv()
    columns_of(first, 0)
    proxies(0, range(NEAR))
    fit_box(0)
    send_own(0)
    fit_box(1)
    send_own(1)
    answer()
    fit_box(2)
    send_own(2)
    fit_box(3)
    send_own(3)
    early(0)
    stage_blocks.wait()
    left_box(0)
    early(1)
    left_box(1)
    late(0)
    early(2)
    left_box(2)
    late(1)
    early(3)
    left_box(3)
    late(2)
    pair_of(0)
    pair_of(1)
    late(3)
    taken()

    base = 16 * home + 8 * side_hi - 16

    def level_one(own):
        for index in range(NEAR):
            box = within(v.near[index, first + own] - base, 10 * MINE)
            lanes = slice(index * PANELS, (index + 1) * PANELS)
            left = (v.left_high[own, :, lanes], v.left_low[own, :, lanes])
            lanes = slice(index * SLOTS, (index + 1) * SLOTS)
            v.cross_high[own, :, lanes], v.cross_low[own, :, lanes] = halves(dot3(left, halves(v.reach[box]), NT))
        v.one[own] = v.block[own] - square((v.cross_high[own], v.cross_low[own]), NT)

    def level_two(j):
        between = v.pair[j]
        v.merged[j, :SLOTS, :SLOTS] = v.one[2 * j]
        v.merged[j, :SLOTS, SLOTS:] = between
        v.merged[j, SLOTS:, :SLOTS] = between.T
        v.merged[j, SLOTS:, SLOTS:] = v.one[2 * j + 1]
        body = halves(v.merged[j])
        which = 2 * member + j
        row, count = v.heard[0, pl.ds(which, 1), :], v.heard[0, pl.ds(8 + which, 1), :]
        for at in range(1, W):
            row = row + v.heard[at, pl.ds(which, 1), :]
            count = count + v.heard[at, pl.ds(8 + which, 1), :]
        columns = chosen_columns(row.astype(jnp.int32), count.astype(jnp.int32))
        gram, right, pick = normal(square(body, TN), columns)
        (fit,) = refine([gram], [right], [pick])
        fit = halves(fit)
        v.two[j] = dot3(halves(dot3(fit, body, NN)), fit, NT)

    mine_one = one_out.at[pl.ds(MINE * member, MINE)]

    def one_rows(target):
        return v.one.at[:, pl.ds(pl.multiple_of(target * ROWS, ROWS), ROWS), :]

    own_one = pltpu.make_async_copy(one_rows(member), mine_one, v.own_sem.at[6])
    ones = [
        send(one_rows(peer[1]), mine_one, v.row_send_sem.at[i], v.row_recv_sem.at[i], peer)
        for i, peer in enumerate(members)
    ]

    up, down = line[0], line[-1]
    half = ROWS // 2
    lines = ((v.lines00, v.lines01), (v.lines10, v.lines11))

    def two_rows(j, part, target):
        return v.two.at[j, pl.ds(pl.multiple_of(target * ROWS + part * half, half), half), :]

    def member_copies(j, part):
        spot = lines[j][part].at[along, member]
        return [
            send(
                two_rows(j, part, peer[1]),
                spot,
                v.block_send_sem.at[2 * j + part, i],
                v.block_recv_sem.at[2 * j + part, i],
                peer,
            )
            for i, peer in enumerate(members)
        ]

    def upward(j, part, step):
        spot = lines[j][part].at[lax.rem(along - step + Z, Z)]
        return send(spot, spot, v.up_send_sem.at[2 * j + part, step], v.up_recv_sem.at[2 * j + part, step], up)

    def downward(j, part, step):
        spot = lines[j][part].at[lax.rem(along + step, Z)]
        return send(spot, spot, v.down_send_sem.at[2 * j + part, step], v.down_recv_sem.at[2 * j + part, step], down)

    def ways(part):
        return ((upward, 4), (downward, 3)) if part == 0 else ((upward, 3), (downward, 4))

    def share(j):
        for part in range(2):
            lines[j][part][along, member] = v.two[
                j, pl.ds(pl.multiple_of(member * ROWS + part * half, half), half), :
            ]
            begin(member_copies(j, part))

    def gather(j, part, step):
        if step == 0:
            for copy in member_copies(j, part):
                copy.wait_recv()
        for copy, count in ways(part):
            if 0 < step <= count:
                copy(j, part, step - 1).wait_recv()
            if step < count:
                copy(j, part, step).start()

    def pack(part, at):
        for s in range(8):
            parent = v.owners[at, s]
            z, m = lax.rem(parent // 16, Z), lax.rem(parent // 2, MEMBERS)
            odd = lax.rem(parent, 2)
            v.packed[part, at, s] = jnp.where(odd == 1, lines[1][part][z, m], lines[0][part][z, m])

    def across_copy(part, i):
        at, peer = plane[i]
        return send(
            v.packed.at[part, at],
            arrived.at[part, across],
            v.plane_send_sem.at[part, i],
            v.plane_recv_sem.at[part, i],
            peer,
        )

    own_across = [
        pltpu.make_async_copy(v.packed.at[part, across], arrived.at[part, across], v.own_sem.at[7 + part])
        for part in range(2)
    ]

    def send_across(part):
        for i, (at, _) in enumerate(plane):
            pack(part, at)
            across_copy(part, i).start()
        pack(part, across)
        own_across[part].start()

    for copy in answers:
        copy.wait_recv()
    level_one(0)
    level_one(1)
    level_two(0)
    share(0)
    level_one(2)
    level_one(3)
    level_two(1)
    share(1)
    begin(ones + [own_one])
    listing.wait()
    gather(0, 0, 0)
    gather(1, 0, 0)
    gather(0, 0, 1)
    gather(1, 0, 1)
    gather(0, 1, 0)
    gather(1, 1, 0)
    gather(0, 0, 2)
    gather(1, 0, 2)
    gather(0, 1, 1)
    gather(1, 1, 1)
    gather(0, 0, 3)
    gather(1, 0, 3)
    gather(0, 1, 2)
    gather(1, 1, 2)
    gather(0, 0, 4)
    gather(1, 0, 4)
    send_across(0)
    gather(0, 1, 3)
    gather(1, 1, 3)
    gather(0, 1, 4)
    gather(1, 1, 4)
    send_across(1)

    for part in range(2):
        for i in range(W - 1):
            across_copy(part, i).wait()
    for copy in own_across + [own_one] + ones:
        copy.wait()
    sent()
    for copy in halos + tables + answers:
        copy.wait_send()
    for j in range(2):
        for part in range(2):
            for copy in member_copies(j, part):
                copy.wait_send()
            for copy, count in ways(part):
                for step in range(count):
                    copy(j, part, step).wait_send()


def place_kernel(owners, one, arrived, one_out, two_out, sems):
    copies = [pltpu.make_async_copy(one, one_out, sems.at[16])]
    for s in range(8):
        source = owners[s] // 8
        at = 2 * (source // 16) + lax.rem(source, 2)
        for part in range(2):
            half = ROWS // 2
            copies.append(
                pltpu.make_async_copy(
                    arrived.at[part, at, s], two_out.at[s, pl.ds(part * half, half), :], sems.at[2 * s + part]
                )
            )
    for copy in copies:
        copy.start()
    for copy in copies:
        copy.wait()


def local(panels, self_blocks, neighbors, skeleton_one, count_one, skeleton_two, count_two, parent_at_slot):
    hbm = pl.BlockSpec(memory_space=pl.ANY)
    vmem = pl.BlockSpec(memory_space=pltpu.VMEM)
    smem = pl.BlockSpec(memory_space=pltpu.SMEM)
    one, arrived = pl.pallas_call(
        kernel,
        out_shape=[
            jax.ShapeDtypeStruct((BOXES, ROWS, SLOTS), F32),
            jax.ShapeDtypeStruct((2, W, 8, ROWS // 2, SLOTS), F32),
        ],
        in_specs=[hbm, hbm, hbm, vmem, smem, vmem, smem, smem],
        out_specs=[hbm, hbm],
        scratch_shapes=[
            pltpu.SMEM((NEAR, BOXES), jnp.int32),
            pltpu.SMEM((W, SLOTS), jnp.int32),
            *(pltpu.VMEM(shape, dtype) for _, shape, dtype in SCRATCH),
            *(pltpu.SemaphoreType.DMA(shape) for _, shape in COPIES),
        ],
        compiler_params=pltpu.CompilerParams(collective_id=0, has_side_effects=True, vmem_limit_bytes=56 * MIB),
        name="skeletonize",
    )(panels, self_blocks, neighbors.T, skeleton_one, count_one, skeleton_two, count_two, parent_at_slot)
    return pl.pallas_call(
        place_kernel,
        out_shape=[
            jax.ShapeDtypeStruct((BOXES, ROWS, SLOTS), F32),
            jax.ShapeDtypeStruct((8, ROWS, SLOTS), F32),
        ],
        in_specs=[smem, hbm, hbm],
        out_specs=[vmem, vmem],
        scratch_shapes=[pltpu.SemaphoreType.DMA((17,))],
        compiler_params=pltpu.CompilerParams(vmem_limit_bytes=56 * MIB),
        name="place",
    )(parent_at_slot, one, arrived)


def solution(mesh):
    placed = (
        P("box", None, None),
        P("box", None, None),
        P("box", None),
        P("box", None),
        P("box"),
        P("box", None),
        P("box"),
        P("box"),
    )
    return jax.shard_map(
        local,
        mesh=mesh,
        in_specs=placed,
        out_specs=(P("box", "blk", None), P("box", "blk", None)),
        check_vma=False,
    )
```

time: 92.1 us -> 86.9 us (0.944); the launches traced: 90.3 us -> 86.7 us
  local copies, waits for them, and re-layouts: 4.59 us -> 0 us
    unnamed x3 -> x0, local copies, waits for them, and re-layouts: 4.59 us -> none
    pallas_call x0 -> x1, Pallas kernels: none -> 2.53 us  [local(): pl.pallas_call(place_kernel, out_shape=[jax.ShapeDtypeStruct((BOXES, ROWS...]
    pallas_call x1, Pallas kernels: 85.1 us -> 83.4 us  [local(): pl.pallas_call(kernel, out_shape=[jax.ShapeDtypeStruct((BOXES, ROWS, SLOT...]
where the time goes in v4:
time: 86.9 us; the launch traced here: 86.7 us
  Pallas kernels  85.9 us (99%)
    pallas_call x1, Pallas kernels, local(): pl.pallas_call(kernel, out_shape=[jax.ShapeDtypeStruct((BOXES, ROWS, SLOT...  83.4 us
    pallas_call x1, Pallas kernels, local(): pl.pallas_call(place_kernel, out_shape=[jax.ShapeDtypeStruct((BOXES, ROWS...  2.53 us

profile of v4, /device:TPU:2, one launch (start us, length us, event | category | flops | bytes accessed | tf_op | source)
XLA Modules:
  0.0 86.7 jit_solution(16311393700270218295)
XLA Ops:
  0.6 83.4 %skeletonize.1 = (f32[16,32,128]{2,1,0:T(8,128)}, f32[2,8,8,16,128]{4,3,2,1,0:T(8,128)}) custom-call(f32[16,4,256]{2,1,0:T(4,128)} %panels.1, f32[16,256,256]{2,1,0:T(8,128)} %self_blocks.1, s32[8,16]{1,0:T(8,128)} %bitcast.1, s32[16,128]{1,0:T(8,128)} %skeleton_one.1, s32[16]{0:T(128)} %count_one.1, s32[8,128]{1,0:T(8,128)} %skeleton_two.1, s32[8]{0:T(128)} %count_two.1, ...), custom_call_target="tpu_custom_call" | custom-call | tf_op jit(solution)/shard_map/skeletonize/pallas_call | solution.py:653
  84.0 2.5 %place.1 = (f32[16,32,128]{2,1,0:T(8,128)}, f32[8,32,128]{2,1,0:T(8,128)}) custom-call(s32[8]{0:T(128)} %owners.1, f32[16,32,128]{2,1,0:T(8,128)} %get-tuple-element.4.one, f32[2,8,8,16,128]{4,3,2,1,0:T(8,128)} %get-tuple-element.5.arrived), custom_call_target="tpu_custom_call" | custom-call | tf_op jit(solution)/shard_map/place/pallas_call | solution.py:670

commit v5 on v4

--- a/solution.py
+++ b/solution.py
@@ -47,13 +47,6 @@
 def place():
     home, member = lax.axis_index("box"), lax.axis_index("blk")
     return home, member
-
-
-def enter(peers):
-    barrier = pltpu.get_barrier_semaphore()
-    for peer in peers:
-        pl.semaphore_signal(barrier, inc=1, device_id=peer, device_id_type=MESH)
-    pl.semaphore_wait(barrier, len(peers))
 
 
 def send(source, target, send_sem, recv_sem, peer):
@@ -116,6 +109,8 @@
 
 
 SCRATCH = [
+    ("skeleton_one", (BOXES, SLOTS), jnp.int32),
+    ("skeleton_two", (8, SLOTS), jnp.int32),
     ("window", (3 * BOXES, 4, PANELS), F32),
     ("column", (2, 3, PANELS, SLOTS), F32),
     ("couples", (MINE + 2, 2 * PANELS, NEAR * PANELS), BF16),
@@ -148,8 +143,8 @@
     ("packed", (2, W, 8, ROWS // 2, SLOTS), F32),
 ]
 COPIES = [
-    ("own", (9,)),
-    ("halo_send", (2,)), ("halo_recv", (2,)),
+    ("own", (9,)), ("stage", (2,)),
+    ("halo_send", (2, 4)), ("halo_recv", (2, 4)),
     ("send", (7, MINE)), ("recv", (6, MINE)), ("give", (5, MINE)), ("take", (5, MINE)),
     ("table_send", (2, 7)), ("table_recv", (2, 7)), ("answer_send", (7,)), ("answer_recv", (7,)),
     ("row_send", (3,)), ("row_recv", (3,)), ("block_send", (4, 3)), ("block_recv", (4, 3)),
@@ -187,12 +182,38 @@
     members = [(home, lax.rem(member + d, MEMBERS)) for d in range(1, MEMBERS)]
     line, plane, across, along = lines_of(home, member)
 
+    barrier = pltpu.get_barrier_semaphore()
+    peers = [after, before, cross, above, below] + members + line + [peer for _, peer in plane]
+    for peer in peers:
+        pl.semaphore_signal(barrier, inc=1, device_id=peer, device_id_type=MESH)
+
     stage_near = pltpu.make_async_copy(neighbors, v.near, v.own_sem.at[0])
     stage_blocks = pltpu.make_async_copy(self_blocks.at[pl.ds(first, MINE)], v.blocks, v.own_sem.at[1])
     stage_panels = pltpu.make_async_copy(panels, v.window.at[pl.ds(BOXES, BOXES)], v.own_sem.at[2])
-    stage_near.start()
-    stage_panels.start()
-    stage_blocks.start()
+    stage_two = pltpu.make_async_copy(skeleton_two, v.skeleton_two, v.stage_sem.at[0])
+    stage_one = pltpu.make_async_copy(skeleton_one, v.skeleton_one, v.stage_sem.at[1])
+    for copy in (stage_near, stage_panels, stage_two, stage_one, stage_blocks):
+        copy.start()
+
+    pl.semaphore_wait(barrier, len(peers))
+
+    def halo(way, piece):
+        boxes_of = pl.ds(MINE * piece, MINE)
+        room = pl.ds(2 * BOXES * way + MINE * piece, MINE)
+        return send(
+            panels.at[boxes_of],
+            v.window.at[room],
+            v.halo_send_sem.at[way, piece],
+            v.halo_recv_sem.at[way, piece],
+            (after, before)[way],
+        )
+
+    def halos(act):
+        for piece in range(MEMBERS):
+            pl.when(piece >= member)(lambda: act(halo(0, piece)))
+            pl.when(piece <= member)(lambda: act(halo(1, piece)))
+
+    halos(lambda copy: copy.start())
 
     lane = lax.broadcasted_iota(jnp.int32, (1, SLOTS), 1)
     nothing = jnp.full((1, SLOTS), -1.0, F32)
@@ -201,20 +222,12 @@
         owner_row = jnp.where(lane == 8 * along + s, parent_at_slot[s].astype(F32), owner_row)
         plain_row = jnp.where(lane == s, parent_at_slot[s], plain_row)
         count_row = jnp.where(lane == 8 * along + s, count_two[s].astype(F32), count_row)
-    v.mine[0:8, :] = skeleton_two[...].astype(F32)
+    stage_two.wait()
+    v.mine[0:8, :] = v.skeleton_two[...].astype(F32)
     v.mine[8:9, :] = owner_row
     v.mine[9:10, :] = count_row
     v.mine[10:16, :] = jnp.zeros((6, SLOTS), F32)
     v.ours[...] = jnp.broadcast_to(plain_row, (8, SLOTS))
-
-    enter([after, before, cross, above, below] + members + line + [peer for _, peer in plane])
-
-    halos = [
-        send(panels, v.window.at[pl.ds(0, BOXES)], v.halo_send_sem.at[0], v.halo_recv_sem.at[0], after),
-        send(panels, v.window.at[pl.ds(2 * BOXES, BOXES)], v.halo_send_sem.at[1], v.halo_recv_sem.at[1], before),
-    ]
-    for copy in halos:
-        copy.start()
 
     spots = [(v.mine, v.line_tables.at[along]), (v.ours, v.plane_tables.at[across])]
     stage_tables = [pltpu.make_async_copy(*spot, v.own_sem.at[3 + i]) for i, spot in enumerate(spots)]
@@ -389,7 +402,7 @@
 
     def fit_box(i):
         box, spot, room = order[i]
-        more = i + 1 < len(order)
+        more = 0 < i < len(order) - 1
         if more:
             columns_of(order[i + 1][0], (i + 1) % 2)
         total = products(room, 0)
@@ -399,7 +412,7 @@
         if more:
             proxies(i + 1, (3, 4, 5))
         low = total[PANELS:]
-        columns = chosen_columns(skeleton_one[pl.ds(box, 1), :], count_one[box])
+        columns = chosen_columns(v.skeleton_one[pl.ds(box, 1), :], count_one[box])
         gram, right, pick = normal(total[:PANELS] + (low + low.T), columns)
         (fit,) = refine([gram], [right], [pick])
         if more:
@@ -428,33 +441,35 @@
         v.pair[j] = dot3(halves(part), split_fit(e), NT)
 
     stage_near.wait()
+    stage_one.wait()
     stage_panels.wait()
-    for copy in halos:
-        copy.wait_recv()
+    halos(lambda copy: copy.wait_recv())
     columns_of(first, 0)
     proxies(0, range(NEAR))
     fit_box(0)
     send_own(0)
+    columns_of(first + 1, 1)
+    proxies(1, range(NEAR))
     fit_box(1)
     send_own(1)
+    early(0)
     answer()
     fit_box(2)
     send_own(2)
+    early(1)
+    late(0)
     fit_box(3)
     send_own(3)
-    early(0)
+    early(2)
+    late(1)
     stage_blocks.wait()
     left_box(0)
-    early(1)
     left_box(1)
-    late(0)
-    early(2)
-    left_box(2)
-    late(1)
     early(3)
-    left_box(3)
     late(2)
     pair_of(0)
+    left_box(2)
+    left_box(3)
     pair_of(1)
     late(3)
     taken()
@@ -617,7 +632,8 @@
     for copy in own_across + [own_one] + ones:
         copy.wait()
     sent()
-    for copy in halos + tables + answers:
+    halos(lambda copy: copy.wait_send())
+    for copy in tables + answers:
         copy.wait_send()
     for j in range(2):
         for part in range(2):
@@ -656,7 +672,7 @@
             jax.ShapeDtypeStruct((BOXES, ROWS, SLOTS), F32),
             jax.ShapeDtypeStruct((2, W, 8, ROWS // 2, SLOTS), F32),
         ],
-        in_specs=[hbm, hbm, hbm, vmem, smem, vmem, smem, smem],
+        in_specs=[hbm, hbm, hbm, hbm, smem, hbm, smem, smem],
         out_specs=[hbm, hbm],
         scratch_shapes=[
             pltpu.SMEM((NEAR, BOXES), jnp.int32),

time: 86.9 us -> 84.6 us (0.974)
  Pallas kernels: 85.9 us -> 83.7 us
    pallas_call x1, Pallas kernels: 83.4 us -> 81.1 us  [local(): pl.pallas_call(kernel, out_shape=[jax.ShapeDtypeStruct((BOXES, ROWS, SLOT...]
where the time goes in v5:
time: 84.6 us; the launch traced here: 84.5 us
  Pallas kernels  83.7 us (99%)
    pallas_call x1, Pallas kernels, local(): pl.pallas_call(kernel, out_shape=[jax.ShapeDtypeStruct((BOXES, ROWS, SLOT...  81.1 us
    pallas_call x1, Pallas kernels, local(): pl.pallas_call(place_kernel, out_shape=[jax.ShapeDtypeStruct((BOXES, ROWS...  2.53 us

profile of v5, /device:TPU:2, one launch (start us, length us, event | category | flops | bytes accessed | tf_op | source)
XLA Modules:
  0.0 84.5 jit_solution(991250439451039900)
XLA Ops:
  0.6 81.1 %skeletonize.1 = (f32[16,32,128]{2,1,0:T(8,128)}, f32[2,8,8,16,128]{4,3,2,1,0:T(8,128)}) custom-call(f32[16,4,256]{2,1,0:T(4,128)} %panels.1, f32[16,256,256]{2,1,0:T(8,128)} %self_blocks.1, s32[8,16]{1,0:T(8,128)} %bitcast.1, s32[16,128]{1,0:T(8,128)} %skeleton_one.1, s32[16]{0:T(128)} %count_one.1, s32[8,128]{1,0:T(8,128)} %skeleton_two.1, s32[8]{0:T(128)} %count_two.1, ...), custom_call_target="tpu_custom_call" | custom-call | tf_op jit(solution)/shard_map/skeletonize/pallas_call | solution.py:669
  81.8 2.5 %place.1 = (f32[16,32,128]{2,1,0:T(8,128)}, f32[8,32,128]{2,1,0:T(8,128)}) custom-call(s32[8]{0:T(128)} %owners.1, f32[16,32,128]{2,1,0:T(8,128)} %get-tuple-element.4.one, f32[2,8,8,16,128]{4,3,2,1,0:T(8,128)} %get-tuple-element.5.arrived), custom_call_target="tpu_custom_call" | custom-call | tf_op jit(solution)/shard_map/place/pallas_call | solution.py:686

commit v6 on v5

--- a/solution.py
+++ b/solution.py
@@ -457,17 +457,17 @@
     fit_box(2)
     send_own(2)
     early(1)
-    late(0)
     fit_box(3)
     send_own(3)
     early(2)
-    late(1)
+    late(0)
     stage_blocks.wait()
     left_box(0)
+    late(1)
+    early(3)
     left_box(1)
-    early(3)
+    pair_of(0)
     late(2)
-    pair_of(0)
     left_box(2)
     left_box(3)
     pair_of(1)

time: 84.6 us -> 83.4 us (0.986)
  Pallas kernels: 83.7 us -> 82.5 us
    pallas_call x1, Pallas kernels: 81.1 us -> 79.9 us  [local(): pl.pallas_call(kernel, out_shape=[jax.ShapeDtypeStruct((BOXES, ROWS, SLOT...]
where the time goes in v6:
time: 83.4 us; the launch traced here: 83.3 us
  Pallas kernels  82.5 us (99%)
    pallas_call x1, Pallas kernels, local(): pl.pallas_call(kernel, out_shape=[jax.ShapeDtypeStruct((BOXES, ROWS, SLOT...  79.9 us
    pallas_call x1, Pallas kernels, local(): pl.pallas_call(place_kernel, out_shape=[jax.ShapeDtypeStruct((BOXES, ROWS...  2.53 us

profile of v6, /device:TPU:2, one launch (start us, length us, event | category | flops | bytes accessed | tf_op | source)
XLA Modules:
  0.0 83.3 jit_solution(4151125870099371462)
XLA Ops:
  0.6 79.9 %skeletonize.1 = (f32[16,32,128]{2,1,0:T(8,128)}, f32[2,8,8,16,128]{4,3,2,1,0:T(8,128)}) custom-call(f32[16,4,256]{2,1,0:T(4,128)} %panels.1, f32[16,256,256]{2,1,0:T(8,128)} %self_blocks.1, s32[8,16]{1,0:T(8,128)} %bitcast.1, s32[16,128]{1,0:T(8,128)} %skeleton_one.1, s32[16]{0:T(128)} %count_one.1, s32[8,128]{1,0:T(8,128)} %skeleton_two.1, s32[8]{0:T(128)} %count_two.1, ...), custom_call_target="tpu_custom_call" | custom-call | tf_op jit(solution)/shard_map/skeletonize/pallas_call | solution.py:669
  80.6 2.5 %place.1 = (f32[16,32,128]{2,1,0:T(8,128)}, f32[8,32,128]{2,1,0:T(8,128)}) custom-call(s32[8]{0:T(128)} %owners.1, f32[16,32,128]{2,1,0:T(8,128)} %get-tuple-element.4.one, f32[2,8,8,16,128]{4,3,2,1,0:T(8,128)} %get-tuple-element.5.arrived), custom_call_target="tpu_custom_call" | custom-call | tf_op jit(solution)/shard_map/place/pallas_call | solution.py:686
